TPU v7x, 256 devices: a whole 4x4x8 slice. The times are simulated.
256 devices in a mesh: hst: 64 (over y, z, core), grp: 4 (over x).
Axes of the slice: x: 4, y: 4, z: 8, core: 2. Of those that a mesh axis runs over, the one named last changes fastest.
Arguments:
- queries: bfloat16 [131072, 1536], P(('hst', 'grp')), may hold values from -5 to 5
- keys_values: bfloat16 [2, 131072, 1536], P(None, ('hst', 'grp')), may hold values from -5 to 5
- token_ids: int32 [131072], replicated, may hold values from 0 to 4095
- lengths: int32 [256], replicated, may hold values from 1 to 512, 98304 in all
- suffix_queries: bfloat16 [1024, 1536], P('hst', 'grp'), may hold values from -5 to 5
- suffix_kv: bfloat16 [2, 1024, 1536], P(None, 'hst', 'grp'), may hold values from -5 to 5
Outputs:
- context_out: bfloat16 [131072, 1536], P(('hst', 'grp'))
- suffix_out: bfloat16 [1024, 1536], P('hst', 'grp')
All inputs are finite; a program needn't handle non-finite values.
Results may differ from a plain program's by a relative error of at most 0.0029.
Values may be sent and summed in bfloat16 or wider, within the bound.
A program may use at most 128 MiB of HBM per device.

v0:
```python
import math

import jax
import jax.numpy as jnp
from jax import lax
from jax.sharding import PartitionSpec as P

HSZ = 128
NAMB = 512


NEG = -1e30


def broadcast(block, axis, owner):
    block = jnp.where(lax.axis_index(axis) == owner, block, jnp.zeros_like(block))
    return lax.psum(block, axis)


def attend(q, keys, values, valid):
    scale = 1.0 / math.sqrt(HSZ)
    s = jnp.einsum("qhd,khd->hqk", q, keys, preferred_element_type=jnp.float32) * scale
    masked = jnp.where(valid[None], s, NEG)
    top = jnp.max(masked, axis=-1)
    weights = jnp.where(valid[None], jnp.exp(masked - top[..., None]), 0.0)
    total = jnp.sum(weights, axis=-1)
    mixed = jnp.einsum(
        "hqk,khd->qhd", weights.astype(jnp.bfloat16), values, preferred_element_type=jnp.float32
    )
    return (top.T, total.T, mixed)


def per_device(queries, keys_values, token_ids, lengths, suffix_queries, suffix_kv):
    groups = lax.axis_size("grp")
    host = lax.axis_index("hst")
    block = host * groups + lax.axis_index("grp")
    rows = queries.shape[0]
    heads = queries.shape[1] // HSZ
    places = jnp.arange(rows)
    clear = token_ids >= NAMB
    swapped = lax.all_to_all(keys_values, "grp", split_axis=2, concat_axis=1, tiled=True)
    anchor = broadcast(keys_values, ("hst", "grp"), 0)
    gathered = lax.all_gather(suffix_queries, "hst", axis=0, tiled=True)
    anchor_ok = clear[:rows] & (places < lengths[0]) & (block > 0)
    own_len = lengths[block]
    own_ok = lax.dynamic_slice_in_dim(clear, block * rows, rows, 0) & (places < own_len)
    causal = places[None, :] <= places[:, None]
    own_valid = causal & (own_ok[None, :] | (places[None, :] == places[:, None]))
    valid = jnp.concatenate([jnp.broadcast_to(anchor_ok[None, :], (rows, rows)), own_valid], axis=1)
    both = jnp.concatenate([anchor, keys_values], axis=1).reshape(2, 2 * rows, heads, HSZ)
    top, total, mixed = attend(queries.reshape(rows, heads, HSZ), both[0], both[1], valid)
    context = mixed / total[:, :, None]
    context = jnp.where((places < own_len)[:, None, None], context, 0.0)
    context_out = context.astype(jnp.bfloat16).reshape(rows, heads * HSZ)
    local_width = suffix_queries.shape[1]
    local_heads = local_width // HSZ
    share = suffix_queries.shape[0]
    span = swapped.shape[1]
    lens = lax.dynamic_slice_in_dim(lengths, host * groups, groups, 0)
    ctx_ok = lax.dynamic_slice_in_dim(clear, host * span, span, 0) & (
        jnp.arange(span) % rows < jnp.repeat(lens, rows, total_repeat_length=span)
    )
    spos = host * share + jnp.arange(share)
    suffix_keys = jnp.concatenate([swapped, suffix_kv], axis=1).reshape(
        2, span + share, local_heads, HSZ
    )
    total_q = gathered.shape[0]
    width_q = min(512, total_q)

    def one_piece(index):
        q = lax.dynamic_slice_in_dim(gathered, index * width_q, width_q, 0).reshape(
            width_q, local_heads, HSZ
        )
        qpos = index * width_q + jnp.arange(width_q)
        seen = jnp.concatenate(
            [jnp.broadcast_to(ctx_ok[None, :], (width_q, span)), spos[None, :] <= qpos[:, None]],
            axis=1,
        )
        return attend(q, suffix_keys[0], suffix_keys[1], seen)

    tops, totals, parts = lax.map(one_piece, jnp.arange(total_q // width_q))
    tops = tops.reshape(total_q, local_heads)
    totals = totals.reshape(total_q, local_heads)
    parts = parts.reshape(total_q, local_heads, HSZ)
    upper = lax.pmax(tops, "hst")
    factor = jnp.exp(tops - upper)
    scaled_parts = parts * factor[..., None]
    scaled_totals = totals * factor
    acc, summed = lax.psum((scaled_parts, scaled_totals), "hst")
    mine_acc = lax.dynamic_slice_in_dim(acc, host * share, share, 0)
    mine_sum = lax.dynamic_slice_in_dim(summed, host * share, share, 0)
    suffix = mine_acc / mine_sum[..., None]
    suffix_out = suffix.astype(jnp.bfloat16).reshape(share, local_width)
    return (context_out, suffix_out)


def solution(mesh):
    return jax.shard_map(
        per_device,
        mesh=mesh,
        in_specs=(
            P(("hst", "grp"), None),
            P(None, ("hst", "grp"), None),
            P(),
            P(),
            P("hst", "grp"),
            P(None, "hst", "grp"),
        ),
        out_specs=(P(("hst", "grp"), None), P("hst", "grp")),
        check_vma=False,
    )
```

profile of v0, /device:TPU:32, one launch (start us, length us, event | category | flops | bytes accessed | tf_op | source)
XLA Modules:
  0.0 903.4 jit_solution(10883413822352663206)
XLA Ops:
  8.0 8.7 copy.36
  16.7 4.7 all-to-all-start
  21.4 0.0 all-reduce.3.cloned.1.call-start
  21.4 3.2 copy.30
  24.7 1.9 broadcast_select_fusion
  26.6 0.0 all-reduce.3.cloned.1.call-update
  26.6 0.0 copy-start.8
  26.6 0.0 copy-start.9
  26.6 0.0 copy-start.10
  26.6 0.0 all-reduce.5.cloned.1.call-start
  26.7 1.1 broadcast_compare_fusion.1
  27.8 0.0 copy-done.5
  27.8 0.2 copy.48
  28.0 2.6 copy.32
  30.6 0.0 copy-done.11
  30.6 0.1 dynamic_slice.28
  30.7 0.7 fusion.53
  31.3 1.4 fusion.49
  32.8 0.7 iota_compare_fusion.3
  33.5 0.7 fusion.54
  34.1 57.4 %all_gather.3 = bf16[1024,384]{1,0:T(8,128)(2,1)} all-gather(bf16[16,384]{1,0:T(8,128)(2,1)S(1)} %copy-done.7), channel_id=1, replica_groups=mesh['hst'=64,'grp'=4] {'hst'}, dimensions={0}, use_global_device_ids=true | all-gather | bytes 798720 | tf_op jit(solution)/shard_map/all_gather | solution.py:43
  91.6 0.0 copy-done.8
  91.6 0.0 copy-done.10
  91.6 2.6 fusion.46
  94.2 0.2 fusion.40
  94.3 1.1 pad_add_fusion.1
  95.4 200.8 %all-reduce.3.cloned.1.call-done = bf16[2,512,1536]{1,2,0:T(8,128)(2,1)} async-done(((bf16[2,512,1536]{1,2,0:T(8,128)(2,1)}), bf16[2,512,1536]{1,2,0:T(8,128)(2,1)}) %all-reduce.3.cloned.1.call-update) | async-done | bytes 3145744 | tf_op jit(solution)/shard_map/psum | solution.py:17
  296.2 4.5 pad_maximum_fusion.1
  300.7 18.5 %fusion.55 = (f32[12,512]{1,0:T(8,128)}, bf16[12,512,1024]{1,2,0:T(8,128)(2,1)}) fusion(pred[512,1024]{0,1:T(8,128)(4,1)} %pad_add_fusion.1, bf16[1024,12,128]{0,2,1:T(8,128)(2,1)} %bitcast.98, bf16[512,12,128]{0,2,1:T(8,128)(2,1)} %bitcast.99), kind=kOutput, calls=%fused_computation.74 | convolution fusion | flops 1648362496 | bytes 17850368 | tf_op jit(solution)/shard_map/sub | solution.py:25
  319.2 0.0 all-to-all-done
  319.2 4.3 copy.56
  323.5 4.0 concatenate.23
  327.5 2.2 pad_maximum_fusion
  329.8 3.5 copy.40
  333.2 54.5 %while.16 = (s32[]{:T(128)}, f32[2,512,3]{1,2,0:T(4,128)S(1)}, f32[2,512,3]{1,2,0:T(4,128)S(1)}, f32[2,512,3,128]{3,1,0,2:T(8,128)}, pred[2048]{0:T(1024)(128)(4...) while((s32[]{:T(128)}, f32[2,512,3]{1,2,0:T(4,128)S(1)}, ...), condition=%wide.region_6.7_spmd.clone, body=%wide.region_3.6_spmd.clone.sunk | while | flops 1665472000 | bytes 73544128 | solution.py:81
  333.5 0.6 dynamic_slice.45
  334.7 1.0 constant_dynamic-slice_fusion.3
  335.7 0.2 copy.58
  336.0 0.1 broadcast_compare_fusion.3
  336.1 2.0 pad_add_fusion.3
  338.1 7.6 fusion.73
  345.6 7.7 fusion.75
  353.4 7.2 fusion.74
  360.6 0.6 dynamic_slice.45
  361.9 1.0 constant_dynamic-slice_fusion.3
  362.9 0.2 copy.58
  363.1 0.1 broadcast_compare_fusion.3
  363.2 2.0 pad_add_fusion.3
  365.2 0.0 copy-start
  365.2 0.0 copy-start.2
  365.2 7.6 fusion.73
  372.8 7.7 fusion.75
  380.5 7.2 fusion.74
  387.7 0.0 copy-done.3
  387.7 0.0 copy-start.1
  387.8 0.0 copy-start.12
  387.8 247.1 %pmax.7 = f32[1024,3]{0,1:T(4,128)S(1)} all-reduce(f32[1024,3]{0,1:T(4,128)S(1)} %bitcast.102), channel_id=1, replica_groups=mesh['hst'=64,'grp'=4] {'hst'}, use_global_device_ids=true, to_apply=%region_7.8 | all-reduce | flops 3072 | bytes 24576 | tf_op jit(solution)/shard_map/pmax | solution.py:85
  634.9 3.1 bitcast_multiply_fusion
  638.0 0.0 all-reduce.5.cloned.1.call-update
  638.0 7.6 fusion.37
  645.6 2.6 copy.43
  648.1 246.4 %psum.23 = f32[1024,3]{0,1:T(4,128)S(1)} all-reduce(f32[1024,3]{0,1:T(4,128)S(1)} %get-tuple-element.138), channel_id=1, replica_groups=mesh['hst'=64,'grp'=4] {'hst'}, use_global_device_ids=true, to_apply=%region_9.10 | all-reduce | flops 3072 | bytes 24576 | tf_op jit(solution)/shard_map/psum | solution.py:89
  894.5 0.1 constant_dynamic-slice_fusion.1
  894.6 1.4 copy_bitcast_fusion.1
  (35 shorter events, 0.1 us)
Async XLA Ops:
  16.7 302.5 %all-to-all-start = ((bf16[2,512,1536]{1,0,2:T(2,128)(2,1)}), bf16[2,512,1536]{1,0,2:T(2,128)(2,1)}, u32[]{:S(2)}, u32[]{:S(2)}) async-start(bf16[2,512,1536]{1,0,2:T(2,128)(2,1)} %copy.36), calls=%async_computation | async-start | bytes 6291456 | tf_op jit(solution)/shard_map/all_to_all | solution.py:41
  21.4 274.8 %all-reduce.3.cloned.1.call-start = ((), (), s32[]{:S(2)}) async-start(), calls=%async_computation.1 | async-start | bytes 6291456 | tf_op jit(solution)/shard_map/psum | solution.py:17
  26.6 1.3 copy-start.5
  26.6 4.0 copy-start.11
  26.6 7.6 copy-start.7
  26.6 65.0 %copy-start.8 = (pred[2048]{0:T(1024)(128)(4,1)S(1)}, pred[2048]{0:T(1024)(128)(4,1)}, u32[]{:S(2)}) copy-start(pred[2048]{0:T(1024)(128)(4,1)} %constant.178) | copy-start | bytes 6148
  26.6 65.0 %copy-start.9 = (pred[2048]{0:T(1024)(128)(4,1)S(1)}, pred[2048]{0:T(1024)(128)(4,1)}, u32[]{:S(2)}) copy-start(pred[2048]{0:T(1024)(128)(4,1)} %constant.179) | copy-start | bytes 6148
  26.6 64.9 %copy-start.10 = (pred[2048]{0:T(1024)(128)(4,1)S(1)}, pred[2048]{0:T(1024)(128)(4,1)}, u32[]{:S(2)}) copy-start(pred[2048]{0:T(1024)(128)(4,1)} %constant.180) | copy-start | bytes 6148
  26.6 867.9 %all-reduce.5.cloned.1.call-start = ((), (), s32[]{:S(2)}) async-start(), calls=%async_computation.2 | async-start | bytes 3145728 | tf_op jit(solution)/shard_map/psum | solution.py:89
  329.7 3.5 copy-start.4
  329.8 3.5 copy-start.6
  338.0 7.6 copy-start
  338.0 7.6 copy-start.2
  353.4 7.2 copy-start.3
  365.2 7.6 copy-start
  365.2 7.6 copy-start.2
  380.5 7.2 copy-start.3
  387.7 250.2 %copy-start.1 = (bf16[1,1024,1536]{1,2,0:T(8,128)(2,1)S(1)}, bf16[1,1024,1536]{1,2,0:T(8,128)(2,1)}, u32[]{:S(2)}) copy-start(bf16[1,1024,1536]{1,2,0:T(8,128)(2,1)} %get-tuple-element.145) | copy-start | bytes 9437188
  387.8 250.2 %copy-start.12 = (f32[12,512]{1,0:T(8,128)S(1)}, f32[12,512]{1,0:T(8,128)}, u32[]{:S(2)}) copy-start(f32[12,512]{1,0:T(8,128)} %get-tuple-element.154) | copy-start | bytes 73732
Sparse Core Ops, SparseCore 0:
  27.6 268.5 all-reduce.2
Sparse Core Ops, SparseCore 1:
  638.1 184.2 all-reduce.4
where the time goes:
time: 910 us; the launch traced here: 903 us
  blocking collectives  551 us (61%)
  waiting for transfers between devices  201 us (22%)
  matrix products  56.6 us (6%)
  other arithmetic  38.7 us (4%)
  local copies, waits for them, and re-layouts  34.2 us (4%)
  between operations  15.7 us (2%)
    pmax x1, blocking collectives, per_device(): upper = lax.pmax(tops, 'hst')  247 us
    psum x1, blocking collectives, per_device(): acc, summed = lax.psum((scaled_parts, scaled_totals), 'hst')  246 us
    psum x1, waiting for transfers between devices, broadcast(): return lax.psum(block, axis)  201 us
    all_gather x1, blocking collectives, per_device(): gathered = lax.all_gather(suffix_queries, 'hst', axis=0, tiled=True)  57.4 us
    dot_general x3, matrix products, attend(): jnp.einsum('hqk,khd->qhd', weights.astype(jnp.bfloat16), values, preferre...  23 us
    unnamed x25, local copies, waits for them, and re-layouts  20.5 us
    sub x1, matrix products, attend(): weights = jnp.where(valid[None], jnp.exp(masked - top[..., None]), 0.0)  18.5 us
  transfers between devices with their start and end apart: 3, of which 1 were waited for; matrix products, arithmetic and copies ran while one was open for 5% of the time, Pallas kernels for 0%

commit v1 on v0

v1 whole, which is shorter than its diff:
```python
import math

import jax
import jax.numpy as jnp
from jax import lax
from jax.experimental import pallas as pl
from jax.experimental.pallas import tpu as pltpu
from jax.sharding import PartitionSpec as P

HEADS = 12
HSZ = 128
BLK = 512
HD = HEADS * HSZ
NAMB = 512
NEG = -1e30
FLOOR = -1e29
SCALE2 = math.log2(math.e) / math.sqrt(HSZ)
CODE = 32767.0
SIZES = (4, 4, 8)
NX, NY, NZ = SIZES
GH = HEADS // NX
SHARE = 16
ROWS = NY * NZ * SHARE
YROWS = NZ * SHARE
TQ = 256
NT = (((1,), (1,)), ((), ()))
MESH = pl.DeviceIdType.MESH

DIRS = ((0, 1), (0, -1), (1, 1), (1, -1), (2, 1), (2, -1))
TREES = (
    ((1, 2, 0), (1, 1, 1)),
    ((1, 2, 0), (-1, 1, 1)),
    ((2, 0, 1), (-1, 1, 1)),
    ((2, 0, 1), (1, -1, 1)),
    ((2, 0, 1), (1, -1, -1)),
    ((0, 1, 2), (-1, 1, -1)),
)
MAXDEPTH = 9
NSLAB = 4


def rem(a, n):
    return lax.rem(a, jnp.int32(n))


def tree_root(k):
    axis, sign = DIRS[k]
    root = [0, 0, 0]
    root[axis] = sign % SIZES[axis]
    return root


def tree_plan(k, coords):
    order, signs = TREES[k]
    root = tree_root(k)
    u, depth = [], jnp.int32(1)
    for axis in range(3):
        n = SIZES[axis]
        r = rem(coords[axis] - root[axis] + n, n)
        if signs[axis] < 0:
            r = rem(n - r, n)
        u.append(r)
        depth = depth + jnp.where(r <= n // 2, r, n - r)
    sends = [None] * 6
    for place, axis in enumerate(order):
        n = SIZES[axis]
        there = jnp.bool_(True)
        for later in order[place + 1 :]:
            there = there & (u[later] == 0)
        far = there & (u[axis] < n // 2)
        near = there & ((u[axis] == 0) | (u[axis] > n // 2 + 1))
        plus, minus = (far, near) if signs[axis] > 0 else (near, far)
        sends[2 * axis] = plus
        sends[2 * axis + 1] = minus
    return depth, sends


def kernel(
    q_hbm, kv_hbm, tok_hbm, lens, sq_hbm, skv_hbm,
    ctx_hbm, suf_ref,
    q_v, kv_v, kvs, tok_v, sq_v, ksuf, qbuf, anc, acc1, m1, l1, own2d, bias, abias, sbias,
    codes, stats, ry, rys, codes2, stats2, rx, rxs, codes3, stats3, rz, rzs, obuf,
    in_sem, kvs_send, kvs_recv, sk_send, sk_recv,
    zq_send, zq_recv, yq_send, yq_recv, xq_send, xq_recv, xh_send, xh_recv,
    a_send, a_recv, s_send, s_recv, r_send,
    ry_send, ry_recv, rys_send, rys_recv, rx_send, rx_recv, rz_send, rz_recv,
    out_sem,
):
    hst = lax.axis_index("hst")
    x = lax.axis_index("grp")
    c = rem(hst, 2)
    z = rem(lax.div(hst, 2), NZ)
    y = lax.div(hst, 2 * NZ)
    block = hst * NX + x

    def dev(px, py, pz, pc):
        return ((py * NZ + pz) * 2 + pc, px)

    def xdev(delta):
        return dev(rem(x + delta, NX), y, z, c)

    def ydev(delta):
        return dev(x, rem(y + delta, NY), z, c)

    def zdev(delta):
        return dev(x, y, rem(z + delta, NZ), c)

    sibling = dev(x, y, z, 1 - c)
    neighbours = [xdev(1), xdev(NX - 1), ydev(1), ydev(NY - 1), zdev(1), zdev(NZ - 1)]

    def remote(src, dst, send, recv, to):
        return pltpu.make_async_remote_copy(
            src_ref=src, dst_ref=dst, send_sem=send, recv_sem=recv, device_id=to, device_id_type=MESH
        )

    sblock = (hst + 1 - 2 * c) * NX + x
    loads = [
        pltpu.make_async_copy(sq_hbm, sq_v, in_sem.at[0]),
        pltpu.make_async_copy(q_hbm, q_v, in_sem.at[1]),
        pltpu.make_async_copy(kv_hbm, kv_v, in_sem.at[2]),
        pltpu.make_async_copy(skv_hbm, ksuf.at[:, pl.ds(0, SHARE), :], in_sem.at[3]),
    ]
    for place, b in enumerate((block, sblock, 0)):
        first = pl.multiple_of(lax.div(b, 2) * 8, 8)
        loads.append(
            pltpu.make_async_copy(tok_hbm.at[pl.ds(first, 8), :], tok_v.at[place], in_sem.at[4 + place])
        )
    for copy in loads:
        copy.start()

    barrier = pltpu.get_barrier_semaphore()
    partners = [sibling]
    partners += [xdev(d) for d in range(1, NX)] + [ydev(d) for d in range(1, NY)]
    partners += [zdev(d) for d in range(1, NZ)]
    for partner in partners:
        pl.semaphore_signal(barrier, inc=1, device_id=partner, device_id_type=MESH)
    is_root = block == 0
    greeted = jnp.int32(len(partners))
    for k in range(3, 6):
        rx_, ry_, rz_ = tree_root(k)
        is_it = (x == rx_) & (y == ry_) & (z == rz_) & (c == 1)

        @pl.when(is_root)
        def _():
            pl.semaphore_signal(barrier, inc=1, device_id=dev(rx_, ry_, rz_, 1), device_id_type=MESH)

        @pl.when(is_it)
        def _():
            pl.semaphore_signal(barrier, inc=1, device_id=(0, 0), device_id_type=MESH)

        greeted = greeted + jnp.where(is_root | is_it, 1, 0)
    pl.semaphore_wait(barrier, greeted)

    loads[0].wait()
    qrow = pl.multiple_of((y * NZ + z) * SHARE, SHARE)
    for e in range(GH):
        qbuf[GH * x + e, pl.ds(qrow, SHARE), :] = sq_v[:, e * HSZ : (e + 1) * HSZ]
    zq = []
    for d in range(1, NZ):
        ref = qbuf.at[pl.ds(GH * x, GH), pl.ds(qrow, SHARE), :]
        zq.append(remote(ref, ref, zq_send.at[d - 1], zq_recv.at[d - 1], zdev(d)))
        zq[-1].start()

    kvs_copy = remote(kv_hbm, kvs, kvs_send, kvs_recv, sibling)
    kvs_copy.start()
    sk_copy = remote(skv_hbm, ksuf.at[:, pl.ds(SHARE, SHARE), :], sk_send, sk_recv, sibling)
    sk_copy.start()

    def slab_of(core, j, s):
        return rem(s, 2) * HEADS + 6 * core + 2 * j + lax.div(s, 2)

    def root_copy(k, s):
        core, j = k // 3, k % 3
        px, py, pz = tree_root(k)
        head = 6 * core + 2 * j + lax.div(s, 2)
        src = kv_hbm.at[rem(s, 2), :, pl.ds(pl.multiple_of(head * HSZ, HSZ), HSZ)]
        return remote(
            src, anc.at[slab_of(core, j, s)], r_send.at[k, s], a_recv.at[j, s], dev(px, py, pz, core)
        )

    @pl.when(is_root)
    def _():
        @pl.loop(0, NSLAB)
        def _(s):
            for k in range(6):
                root_copy(k, s).start()

    plans = []
    for j in range(3):
        depth0, sends0 = tree_plan(j, (x, y, z))
        depth1, sends1 = tree_plan(3 + j, (x, y, z))
        first = c == 0
        depth = jnp.where(first, depth0, depth1)
        sends = [(first & s0) | (~first & s1) for s0, s1 in zip(sends0, sends1)]
        plans.append((1 + lax.div(3 * (depth - 1), 2), sends))
    last_step = 1 + 3 * (MAXDEPTH - 1) // 2 + NSLAB

    def tree_copy(j, s, d):
        ref = anc.at[slab_of(c, j, s)]
        return remote(ref, ref, a_send.at[j, s, d], a_recv.at[j, s], neighbours[d])

    def sibling_copy(j, s, core):
        ref = anc.at[slab_of(core, j, s)]
        return remote(ref, ref, s_send.at[j, s], s_recv.at[j, s], sibling)

    def anchor_step(t):
        for j in range(3):
            place, sends = plans[j]
            s = t - place

            @pl.when((s >= 0) & (s < NSLAB))
            def _():
                tree_copy(j, s, 0).wait_recv()
                for d in range(6):

                    @pl.when(sends[d])
                    def _():
                        tree_copy(j, s, d).start()

                sibling_copy(j, s, c).start()

    for copy in loads[4:]:
        copy.wait()
    flat = lax.broadcasted_iota(jnp.int32, (4, HSZ), 0) * HSZ + lax.broadcasted_iota(jnp.int32, (4, HSZ), 1)

    def key_bias(place, b, length, on):
        both = tok_v[place]
        ids = jnp.where(rem(b, 2) == 1, both[4:8], both[0:4])
        part = jnp.where((ids >= NAMB) & (flat < length) & on, 0.0, NEG)
        return jnp.concatenate([part[i : i + 1] for i in range(4)], axis=1)

    own_len = lens[block]
    own_bias = key_bias(0, block, own_len, True)
    bias[:, 0:BLK] = own_bias
    bias[:, BLK:] = key_bias(1, sblock, lens[sblock], True)
    abias[...] = key_bias(2, jnp.int32(0), lens[0], block > 0)
    row2d = lax.broadcasted_iota(jnp.int32, (BLK, BLK), 0)
    col2d = lax.broadcasted_iota(jnp.int32, (BLK, BLK), 1)
    own2d[...] = jnp.where(col2d == row2d, 0.0, jnp.where(col2d < row2d, own_bias, NEG))
    krow = lax.broadcasted_iota(jnp.int32, (ROWS, HSZ), 0)
    klane = lax.broadcasted_iota(jnp.int32, (ROWS, HSZ), 1)
    qpos = lax.div(krow, SHARE) * (2 * SHARE) + c * SHARE + rem(krow, SHARE)
    kpos = jnp.where(klane < SHARE, hst * SHARE + klane, (hst + 1 - 2 * c) * SHARE + klane - SHARE)
    sbias[...] = jnp.where((klane < 2 * SHARE) & (kpos <= qpos), 0.0, NEG)
    ksuf[:, 2 * SHARE :, :] = jnp.zeros((2, HSZ - 2 * SHARE, GH * HSZ), ksuf.dtype)
    stats[...] = jnp.zeros_like(stats)

    def columns(h):
        return pl.ds(pl.multiple_of(h * HSZ, HSZ), HSZ)

    def wide(a, copies):
        return jnp.concatenate([a] * copies, axis=1)

    def pipelined(units, scores, finish):
        ready = scores(*units[0])
        for i, unit in enumerate(units):
            later = scores(*units[i + 1]) if i + 1 < len(units) else None
            finish(*unit, ready)
            ready = later

    def yq_block(py, first, rows):
        return qbuf.at[pl.ds(GH * x, GH), pl.ds(pl.multiple_of(py * YROWS + first, SHARE), rows), :]

    def yq_copy(py, first, rows, sem, delta):
        ref = yq_block(py, first, rows)
        return remote(ref, ref, yq_send.at[sem], yq_recv.at[sem], ydev(delta))

    yq_own = [yq_copy(y, 0, YROWS, 0, 1), yq_copy(y, 0, YROWS, 1, NY - 1)]
    below, above, over = rem(y + NY - 1, NY), rem(y + 1, NY), rem(y + 2, NY)
    yq_in = [yq_copy(below, 0, YROWS, 0, 1), yq_copy(above, 0, YROWS, 1, NY - 1)]
    half = YROWS // 2
    yq_on = [yq_copy(below, 0, half, 2, 1), yq_copy(above, half, half, 3, NY - 1)]
    yq_far = [yq_copy(over, 0, half, 2, 1), yq_copy(over, half, half, 3, NY - 1)]

    def xq_copy(px, e, way):
        ref = qbuf.at[GH * px + e]
        to = dev(rem(x + jnp.where(way == 0, 1, NX - 1), NX), y, z, c)
        return remote(ref, ref, xq_send.at[way, e], xq_recv.at[way, e], to)

    def xh_copy(px, e, way):
        ref = qbuf.at[GH * px + e, pl.ds(pl.multiple_of(way * (ROWS // 2), SHARE), ROWS // 2), :]
        to = dev(rem(x + jnp.where(way == 0, 1, NX - 1), NX), y, z, c)
        return remote(ref, ref, xh_send.at[way, e], xh_recv.at[way, e], to)

    loads[1].wait()
    loads[2].wait()

    def own_scores(h, t):
        q = q_v[t * TQ : (t + 1) * TQ, columns(h)]
        k = kv_v[0, 0 : (t + 1) * TQ, columns(h)]
        s = lax.dot_general(q, k, NT, preferred_element_type=jnp.float32)
        return s + own2d[t * TQ : (t + 1) * TQ, 0 : (t + 1) * TQ]

    def own_finish(h, t, s):
        rows = slice(t * TQ, (t + 1) * TQ)
        m = jnp.max(s, axis=1, keepdims=True)
        p = jnp.exp2((s - m) * SCALE2)
        v = kv_v[1, 0 : (t + 1) * TQ, columns(h)]
        l1[h, rows, :] = jnp.broadcast_to(jnp.sum(p, axis=1, keepdims=True), (TQ, HSZ))
        m1[h, rows, :] = jnp.broadcast_to(m, (TQ, HSZ))
        acc1[h, rows, :] = jnp.dot(p.astype(jnp.bfloat16), v, preferred_element_type=jnp.float32)

    @pl.loop(0, HEADS // 2)
    def _(t):
        @pl.when(t == 2)
        def _():
            for copy in zq:
                copy.wait_recv()
            for copy in yq_own:
                copy.start()

        @pl.when(t == 3)
        def _():
            for arrived, on in zip(yq_in, yq_on):
                arrived.wait_recv()
                on.start()

        @pl.when(t == 4)
        def _():
            for copy in yq_far:
                copy.wait_recv()
            for e in range(GH):
                for way in range(2):
                    xq_copy(x, e, way).start()

        anchor_step(t)
        pipelined([(2 * t + i, tile) for i in range(2) for tile in range(BLK // TQ)], own_scores, own_finish)

    sk_copy.wait_recv()
    loads[3].wait()
    kvs_copy.wait_recv()
    lane = lax.broadcasted_iota(jnp.int32, (TQ, HSZ), 1)

    def encode(o):
        a = jnp.maximum(jnp.max(jnp.abs(o), axis=-1, keepdims=True), 1e-30)
        return a, jnp.round(o * (CODE / a)).astype(jnp.int32).astype(jnp.int16)

    def suffix_head(h, e, own_group):
        def scores(t):
            q = qbuf[h, t * TQ : (t + 1) * TQ, :]
            parts = []
            for i, ref in enumerate((kv_v, kvs)):
                s = lax.dot_general(q, ref[0, :, columns(h)], NT, preferred_element_type=jnp.float32)
                parts.append(s + bias[:, i * BLK : (i + 1) * BLK])
            if own_group:
                s = lax.dot_general(q, ksuf[0, :, columns(e)], NT, preferred_element_type=jnp.float32)
                parts.append(s + sbias[t * TQ : (t + 1) * TQ, :])
            return jnp.concatenate(parts, axis=1)

        def finish(t, s):
            rows = slice(t * TQ, (t + 1) * TQ)
            m = jnp.maximum(jnp.max(s, axis=1, keepdims=True), FLOOR)
            p = jnp.exp2((s - m) * SCALE2)
            l = jnp.maximum(jnp.sum(p, axis=1, keepdims=True), 1.0)
            w = p.astype(jnp.bfloat16)
            o = jnp.dot(w[:, :BLK], kv_v[1, :, columns(h)], preferred_element_type=jnp.float32)
            o = o + jnp.dot(w[:, BLK : 2 * BLK], kvs[1, :, columns(h)], preferred_element_type=jnp.float32)
            if own_group:
                o = o + jnp.dot(w[:, 2 * BLK :], ksuf[1, :, columns(e)], preferred_element_type=jnp.float32)
            a, code = encode(o / l)
            codes[h, rows, :] = code
            lse = m * SCALE2 + jnp.log2(l)
            old = stats[rows, :]
            stats[rows, :] = jnp.where(lane == h, lse, jnp.where(lane == h + HSZ // 2, a, old))

        pipelined([(t,) for t in range(ROWS // TQ)], scores, finish)

    def ry_copy(h, d):
        to_row = pl.multiple_of(rem(y + d, NY) * YROWS, SHARE)
        return remote(
            codes.at[h, pl.ds(to_row, YROWS), :], ry.at[d - 1, h], ry_send.at[d - 1, h], ry_recv.at[d - 1, h], ydev(d)
        )

    @pl.loop(0, GH)
    def _(i):
        anchor_step(HEADS // 2 + i)
        h = GH * x + i
        suffix_head(h, i, True)
        for d in range(1, NY):
            ry_copy(h, d).start()

    @pl.loop(GH, HEADS)
    def _(i):
        anchor_step(HEADS // 2 + i)
        opposite = i >= 3 * GH
        way = rem(i - GH, 2)
        e = jnp.where(opposite, i - 3 * GH, lax.div(i - GH, 2))
        px = jnp.where(opposite, rem(x + 2, NX), rem(x + jnp.where(way == 0, NX - 1, 1), NX))

        @pl.when(jnp.logical_not(opposite))
        def _():
            xq_copy(px, e, way).wait_recv()
            xh_copy(px, e, way).start()

        @pl.when(opposite)
        def _():
            xh_copy(px, e, jnp.int32(0)).wait_recv()
            xh_copy(px, e, jnp.int32(1)).wait_recv()

        h = GH * px + e
        suffix_head(h, e, False)
        for d in range(1, NY):
            ry_copy(h, d).start()

    def rys_copy(d):
        to_row = pl.multiple_of(rem(y + d, NY) * YROWS, SHARE)
        return remote(stats.at[pl.ds(to_row, YROWS), :], rys.at[d - 1], rys_send.at[d - 1], rys_recv.at[d - 1], ydev(d))

    for d in range(1, NY):
        rys_copy(d).start()

    def merge(parts):
        top = parts[0]
        for s in parts[1:]:
            top = jnp.maximum(top, s)
        weights = [jnp.exp2(s - top) for s in parts]
        total = weights[0]
        for w in weights[1:]:
            total = total + w
        inverse = 1.0 / (total * CODE)
        coefficients = [w * inverse * pltpu.roll(s, HSZ // 2, 1) for w, s in zip(weights, parts)]
        return top + jnp.log2(total), coefficients

    def pick(a, h):
        there = lax.broadcasted_iota(jnp.int32, a.shape, 1) == h
        return jnp.sum(jnp.where(there, a, 0.0), axis=1, keepdims=True)

    def blend(coefficients, coded, h):
        total = None
        for coefficient, code in zip(coefficients, coded):
            term = pick(coefficient, h) * code.astype(jnp.int32).astype(jnp.float32)
            total = term if total is None else total + term
        return total

    def reduce_y():
        for d in range(1, NY):
            rys_copy(d).wait_recv()

        @pl.loop(0, HEADS)
        def _(h):
            for d in range(1, NY):
                ry_copy(h, d).wait_recv()

        own_rows = pl.ds(pl.multiple_of(y * YROWS, SHARE), YROWS)
        lse, coefficients = merge([stats[own_rows, :]] + [rys[d] for d in range(NY - 1)])
        stats2[...] = lse
        lanes = lax.broadcasted_iota(jnp.int32, (YROWS, HSZ), 1)

        @pl.loop(0, HEADS)
        def _(h):
            o = blend(coefficients, [codes[h, own_rows, :]] + [ry[d, h] for d in range(NY - 1)], h)
            a, code = encode(o)
            codes2[h] = code
            stats2[...] = jnp.where(lanes == h + HSZ // 2, a, stats2[...])

    def rx_copies(d):
        px = rem(x + d, NX)
        return [
            remote(codes2.at[pl.ds(GH * px, GH)], rx.at[d - 1], rx_send.at[0, d - 1], rx_recv.at[0, d - 1], xdev(d)),
            remote(stats2, rxs.at[d - 1], rx_send.at[1, d - 1], rx_recv.at[1, d - 1], xdev(d)),
        ]

    def reduce_x():
        for d in range(1, NX):
            for copy in rx_copies(d):
                copy.wait_recv()
        lse, coefficients = merge([stats2[...]] + [rxs[d] for d in range(NX - 1)])
        lanes = lax.broadcasted_iota(jnp.int32, (YROWS, HSZ), 1)
        for e in range(GH):
            h = GH * x + e
            o = blend(coefficients, [codes2[h]] + [rx[d, e] for d in range(NX - 1)], h)
            a, code = encode(o)
            codes3[e] = code
            lse = jnp.where(lanes == h + HSZ // 2, a, lse)
        stats3[...] = lse

    def rz_copies(d):
        rows = pl.ds(pl.multiple_of(rem(z + d, NZ) * SHARE, SHARE), SHARE)
        return [
            remote(codes3.at[:, rows, :], rz.at[d - 1], rz_send.at[0, d - 1], rz_recv.at[0, d - 1], zdev(d)),
            remote(stats3.at[rows, :], rzs.at[d - 1], rz_send.at[1, d - 1], rz_recv.at[1, d - 1], zdev(d)),
        ]

    def reduce_z():
        for d in range(1, NZ):
            for copy in rz_copies(d):
                copy.wait_recv()
        rows = pl.ds(pl.multiple_of(z * SHARE, SHARE), SHARE)
        unused, coefficients = merge([stats3[rows, :]] + [rzs[d] for d in range(NZ - 1)])
        for e in range(GH):
            o = blend(coefficients, [codes3[e, rows, :]] + [rz[d, e] for d in range(NZ - 1)], GH * x + e)
            suf_ref[:, e * HSZ : (e + 1) * HSZ] = o.astype(suf_ref.dtype)

    @pl.loop(HEADS // 2 + HEADS, last_step)
    def _(t):
        anchor_step(t)

    @pl.loop(0, NSLAB)
    def _(s):
        for j in range(3):
            sibling_copy(j, s, 1 - c).wait_recv()

    def anchor_scores(h, t):
        q = q_v[t * TQ : (t + 1) * TQ, columns(h)]
        return lax.dot_general(q, anc[h], NT, preferred_element_type=jnp.float32) + abias[...]

    def anchor_finish(h, t, s):
        rows = slice(t * TQ, (t + 1) * TQ)
        before = m1[h, rows, :]
        m = jnp.maximum(before, jnp.max(s, axis=1, keepdims=True))
        p = jnp.exp2((s - wide(m, BLK // HSZ)) * SCALE2)
        fade = jnp.exp2((before - m) * SCALE2)
        l = l1[h, rows, :] * fade + jnp.sum(p, axis=1, keepdims=True)
        o = jnp.dot(p.astype(jnp.bfloat16), anc[HEADS + h], preferred_element_type=jnp.float32)
        o = (acc1[h, rows, :] * fade + o) / l
        place = lax.broadcasted_iota(jnp.int32, (TQ, HSZ), 0) + t * TQ
        obuf[h, rows, :] = jnp.where(place < own_len, o, 0.0).astype(obuf.dtype)

    def out_copy(h):
        return pltpu.make_async_copy(obuf.at[h], ctx_hbm.at[:, columns(h)], out_sem.at[h])

    @pl.loop(0, HEADS // 2)
    def _(t):
        @pl.when(t == 2)
        def _():
            reduce_y()
            for d in range(1, NX):
                for copy in rx_copies(d):
                    copy.start()

        @pl.when(t == 4)
        def _():
            reduce_x()
            for d in range(1, NZ):
                for copy in rz_copies(d):
                    copy.start()

        pipelined([(2 * t + i, tile) for i in range(2) for tile in range(BLK // TQ)], anchor_scores, anchor_finish)
        for i in range(2):
            out_copy(2 * t + i).start()

    reduce_z()

    for copy in zq + yq_own + yq_on + [kvs_copy, sk_copy]:
        copy.wait_send()

    @pl.loop(0, GH)
    def _(e):
        for way in range(2):
            xq_copy(x, e, jnp.int32(way)).wait_send()
            xh_copy(x, e, jnp.int32(way)).wait_send()

    @pl.loop(0, NSLAB)
    def _(s):
        for j in range(3):
            for d in range(6):

                @pl.when(plans[j][1][d])
                def _():
                    tree_copy(j, s, d).wait_send()

            sibling_copy(j, s, c).wait_send()

    @pl.when(is_root)
    def _():
        @pl.loop(0, NSLAB)
        def _(s):
            for k in range(6):
                root_copy(k, s).wait_send()

    @pl.loop(0, HEADS)
    def _(h):
        for d in range(1, NY):
            ry_copy(h, d).wait_send()
        out_copy(h).wait()

    for d in range(1, NY):
        rys_copy(d).wait_send()
    for d in range(1, NX):
        for copy in rx_copies(d):
            copy.wait_send()
    for d in range(1, NZ):
        for copy in rz_copies(d):
            copy.wait_send()


def per_device(queries, keys_values, token_ids, lengths, suffix_queries, suffix_kv):
    bf16, f32, i16 = jnp.bfloat16, jnp.float32, jnp.int16
    dma = pltpu.SemaphoreType.DMA
    scratch = [
        pltpu.VMEM((BLK, HD), bf16),
        pltpu.VMEM((2, BLK, HD), bf16),
        pltpu.VMEM((2, BLK, HD), bf16),
        pltpu.VMEM((3, 8, HSZ), jnp.int32),
        pltpu.VMEM((SHARE, GH * HSZ), bf16),
        pltpu.VMEM((2, HSZ, GH * HSZ), bf16),
        pltpu.VMEM((HEADS, ROWS, HSZ), bf16),
        pltpu.VMEM((2 * HEADS, BLK, HSZ), bf16),
        pltpu.VMEM((HEADS, BLK, HSZ), f32),
        pltpu.VMEM((HEADS, BLK, HSZ), f32),
        pltpu.VMEM((HEADS, BLK, HSZ), f32),
        pltpu.VMEM((BLK, BLK), f32),
        pltpu.VMEM((1, 2 * BLK), f32),
        pltpu.VMEM((1, BLK), f32),
        pltpu.VMEM((ROWS, HSZ), f32),
        pltpu.VMEM((HEADS, ROWS, HSZ), i16),
        pltpu.VMEM((ROWS, HSZ), f32),
        pltpu.VMEM((NY - 1, HEADS, YROWS, HSZ), i16),
        pltpu.VMEM((NY - 1, YROWS, HSZ), f32),
        pltpu.VMEM((HEADS, YROWS, HSZ), i16),
        pltpu.VMEM((YROWS, HSZ), f32),
        pltpu.VMEM((NX - 1, GH, YROWS, HSZ), i16),
        pltpu.VMEM((NX - 1, YROWS, HSZ), f32),
        pltpu.VMEM((GH, YROWS, HSZ), i16),
        pltpu.VMEM((YROWS, HSZ), f32),
        pltpu.VMEM((NZ - 1, GH, SHARE, HSZ), i16),
        pltpu.VMEM((NZ - 1, SHARE, HSZ), f32),
        pltpu.VMEM((HEADS, BLK, HSZ), bf16),
        dma((7,)),
        dma, dma, dma, dma,
        dma((NZ - 1,)), dma((NZ - 1,)),
        dma((4,)), dma((4,)),
        dma((2, GH)), dma((2, GH)),
        dma((2, GH)), dma((2, GH)),
        dma((3, NSLAB, 6)), dma((3, NSLAB)),
        dma((3, NSLAB)), dma((3, NSLAB)),
        dma((6, NSLAB)),
        dma((NY - 1, HEADS)), dma((NY - 1, HEADS)),
        dma((NY - 1,)), dma((NY - 1,)),
        dma((2, NX - 1)), dma((2, NX - 1)),
        dma((2, NZ - 1)), dma((2, NZ - 1)),
        dma((HEADS,)),
    ]
    anywhere = pl.BlockSpec(memory_space=pl.ANY)
    return pl.pallas_call(
        kernel,
        out_shape=(
            jax.ShapeDtypeStruct((BLK, HD), bf16),
            jax.ShapeDtypeStruct((SHARE, GH * HSZ), bf16),
        ),
        in_specs=[anywhere, anywhere, anywhere, pl.BlockSpec(memory_space=pltpu.SMEM), anywhere, anywhere],
        out_specs=(anywhere, pl.BlockSpec(memory_space=pltpu.VMEM)),
        scratch_shapes=scratch,
        compiler_params=pltpu.CompilerParams(
            collective_id=0, has_side_effects=True, vmem_limit_bytes=56 * 2**20
        ),
        cost_estimate=pl.CostEstimate(
            flops=6_500_000_000, bytes_accessed=6_500_000, transcendentals=12_600_000
        ),
        name="star",
    )(queries, keys_values, token_ids.reshape(-1, HSZ), lengths, suffix_queries, suffix_kv)


def solution(mesh):
    return jax.shard_map(
        per_device,
        mesh=mesh,
        in_specs=(
            P(("hst", "grp"), None),
            P(None, ("hst", "grp"), None),
            P(),
            P(),
            P("hst", "grp"),
            P(None, "hst", "grp"),
        ),
        out_specs=(P(("hst", "grp"), None), P("hst", "grp")),
        check_vma=False,
    )
```

time: 910 us -> 98.4 us (0.11)
  blocking collectives: 551 us -> 0 us
  waiting for transfers between devices: 201 us -> 0 us
  Pallas kernels: 0 us -> 92.8 us
  matrix products: 56.6 us -> 0 us
  other arithmetic: 38.7 us -> 0 us
  local copies, waits for them, and re-layouts: 34.2 us -> 3.26 us
  between operations: 15.7 us -> 0.65 us
    pmax x1 -> x0, blocking collectives: 247 us -> none  [per_device(): upper = lax.pmax(tops, 'hst')]
    psum x1 -> x0, blocking collectives: 246 us -> none  [per_device(): acc, summed = lax.psum((scaled_parts, scaled_totals), 'hst')]
    psum x2 -> x0, waiting for transfers between devices: 201 us -> none  [the longest x1 201 us: broadcast(): return lax.psum(block, axis)]
    pallas_call x0 -> x1, Pallas kernels: none -> 92.8 us  [per_device(): pl.pallas_call(kernel, out_shape=(jax.ShapeDtypeStruct((BLK, HD), bf16),...]
    all_gather x1 -> x0, blocking collectives: 57.4 us -> none  [per_device(): gathered = lax.all_gather(suffix_queries, 'hst', axis=0, tiled=True)]
    dot_general x5 -> x0, matrix products: 38.1 us -> none  [the longest x3 23 us: attend(): jnp.einsum('hqk,khd->qhd', weights.astype(jnp.bfloat16), values, preferre...]
    sub x1 -> x0, matrix products: 18.5 us -> none  [attend(): weights = jnp.where(valid[None], jnp.exp(masked - top[..., None]), 0.0)]
    unnamed x25 -> x4, local copies, waits for them, and re-layouts: 20.5 us -> 3.26 us
  transfers between devices with their start and end apart: 3 -> 0, of which waited for: 1 -> 0; matrix products, arithmetic and copies ran while one was open for 5% -> 0% of each run, Pallas kernels for 0% -> 0%
where the time goes in v1:
time: 98.4 us; the launch traced here: 96.7 us
  Pallas kernels  92.8 us (94%)
  local copies, waits for them, and re-layouts  3.26 us (3%)
    pallas_call x1, Pallas kernels, per_device(): pl.pallas_call(kernel, out_shape=(jax.ShapeDtypeStruct((BLK, HD), bf16),...  92.8 us
    unnamed x4, local copies, waits for them, and re-layouts  3.26 us

profile of v1, /device:TPU:32, one launch (start us, length us, event | category | flops | bytes accessed | tf_op | source)
XLA Modules:
  0.0 96.7 jit_solution(12480291230461956653)
XLA Ops:
  0.6 92.8 %star.1 = (bf16[512,1536]{1,0:T(8,128)(2,1)}, bf16[16,384]{1,0:T(8,128)(2,1)}) custom-call(bf16[512,1536]{1,0:T(8,128)(2,1)} %q_hbm.1, bf16[2,512,1536]{2,1,0:T(8,128)(2,1)} %kv_hbm.1, s32[1024,128]{1,0:T(8,128)} %bitcast.1, s32[256]{0:T(256)} %lens.1, bf16[16,384]{1,0:T(8,128)(2,1)} %sq_hbm.1, bf16[2,16,384]{2,1,0:T(8,128)(2,1)} %skv_hbm.1), custom_call_target="tpu_custom_call" | custom-call | flops 6499999744 | bytes 6500000 | tf_op jit(solution)/shard_map/star/pallas_call | solution.py:635
  93.4 0.0 copy-start
  93.4 2.7 %copy.10 = bf16[512,1536]{1,0:T(8,128)(2,1)} copy(bf16[512,1536]{1,0:T(8,128)(2,1)} %get-tuple-element.4) | data formatting | bytes 3145728
  96.1 0.0 copy-done
  96.1 0.6 copy.11
Async XLA Ops:
  93.4 2.7 %copy-start = (bf16[16,384]{1,0:T(8,128)(2,1)S(1)}, bf16[16,384]{1,0:T(8,128)(2,1)}, u32[]{:S(2)}) copy-start(bf16[16,384]{1,0:T(8,128)(2,1)} %get-tuple-element.5) | copy-start | bytes 36868

commit v2 on v0

v2 whole, which is shorter than its diff:
```python
import math

import jax
import jax.numpy as jnp
from jax import lax
from jax.experimental import pallas as pl
from jax.experimental.pallas import tpu as pltpu
from jax.sharding import PartitionSpec as P

HEADS = 12
HSZ = 128
BLK = 512
HD = HEADS * HSZ
NAMB = 512
NEG = -1e30
FLOOR = -1e29
SCALE2 = math.log2(math.e) / math.sqrt(HSZ)
CODE = 32767.0
SIZES = (4, 4, 8)
NX, NY, NZ = SIZES
GH = HEADS // NX
SHARE = 16
QB = NZ * SHARE
TQ = 256
NCH = 3
CW = HD // 2 // NCH
PROWS = BLK // (NX * NY)
AROWS = BLK // NX
NT = (((1,), (1,)), ((), ()))
MESH = pl.DeviceIdType.MESH


def rem(a, n):
    return lax.rem(a, jnp.int32(n))


def kernel(
    q_hbm, kv_hbm, tok_hbm, lens, sq_hbm, skv_hbm,
    ctx_hbm, suf_ref,
    q_v, kv_v, kvs, tok_v, ksuf, qbuf, anc, stage, acc1, m1, l1, own2d, bias, abias,
    codes, stats, rb, rbs, codes2, stats2, ra, ras, codes3, stats3, rz, rzs, turned, obuf,
    in_sem, kvs_send, kvs_recv, sk_send, sk_recv,
    zq_send, zq_recv, bq_send, bq_recv, aq_send, aq_recv,
    sc_send, sc_recv, own_sem, sb_send, sb_recv, zb_send, zb_recv, bb_send, bb_recv, ab_send, ab_recv, sib_send, sib_recv,
    rb_send, rb_recv, ra_send, ra_recv, rz_send, rz_recv,
    out_sem,
):
    hst = lax.axis_index("hst")
    x = lax.axis_index("grp")
    c = rem(hst, 2)
    z = rem(lax.div(hst, 2), NZ)
    y = lax.div(hst, 2 * NZ)
    block = hst * NX + x
    first = c == 0
    ca = jnp.where(first, x, y)
    cb = jnp.where(first, y, x)

    def dev(px, py, pz, pc):
        return ((py * NZ + pz) * 2 + pc, px)

    def place(pa, pb, pz, pc):
        on = pc == 0
        return dev(jnp.where(on, pa, pb), jnp.where(on, pb, pa), pz, pc)

    def adev(delta):
        return place(rem(ca + delta, NX), cb, z, c)

    def bdev(delta):
        return place(ca, rem(cb + delta, NX), z, c)

    def zdev(delta):
        return dev(x, y, rem(z + delta, NZ), c)

    sibling = dev(x, y, z, 1 - c)

    def remote(src, dst, send, recv, to):
        return pltpu.make_async_remote_copy(
            src_ref=src, dst_ref=dst, send_sem=send, recv_sem=recv, device_id=to, device_id_type=MESH
        )

    sblock = (hst + 1 - 2 * c) * NX + x
    zrow = pl.multiple_of(z * SHARE, SHARE)
    qloads = [
        pltpu.make_async_copy(
            sq_hbm.at[:, pl.ds(e * HSZ, HSZ)], qbuf.at[ca, cb, e, pl.ds(zrow, SHARE), :], in_sem.at[6 + e]
        )
        for e in range(GH)
    ]
    loads = [
        pltpu.make_async_copy(q_hbm, q_v, in_sem.at[0]),
        pltpu.make_async_copy(kv_hbm, kv_v, in_sem.at[1]),
        pltpu.make_async_copy(skv_hbm, ksuf.at[:, pl.ds(0, SHARE), :], in_sem.at[2]),
    ]
    for i, b in enumerate((block, sblock, 0)):
        row = pl.multiple_of(lax.div(b, 2) * 8, 8)
        loads.append(pltpu.make_async_copy(tok_hbm.at[pl.ds(row, 8), :], tok_v.at[i], in_sem.at[3 + i]))
    for copy in qloads + loads:
        copy.start()

    barrier = pltpu.get_barrier_semaphore()
    partners = [sibling]
    partners += [adev(d) for d in range(1, NX)] + [bdev(d) for d in range(1, NY)]
    partners += [zdev(d) for d in range(1, NZ)]
    for partner in partners:
        pl.semaphore_signal(barrier, inc=1, device_id=partner, device_id_type=MESH)
    is_root = block == 0
    is_extra = (z == 0) & (x == 0) & (y > 0) & (c == 1)

    @pl.when(is_extra)
    def _():
        pl.semaphore_signal(barrier, inc=1, device_id=(0, 0), device_id_type=MESH)

    pl.semaphore_wait(barrier, len(partners) + jnp.where(is_root, NY - 1, 0))

    for copy in qloads:
        copy.wait()
    zq = []
    for d in range(1, NZ):
        ref = qbuf.at[ca, cb, :, pl.ds(zrow, SHARE), :]
        zq.append(remote(ref, ref, zq_send.at[d - 1], zq_recv.at[d - 1], zdev(d)))
        zq[-1].start()

    kvs_copy = remote(kv_hbm, kvs, kvs_send, kvs_recv, sibling)
    kvs_copy.start()
    sk_copy = remote(skv_hbm, ksuf.at[:, pl.ds(SHARE, SHARE), :], sk_send, sk_recv, sibling)
    sk_copy.start()

    def piece(ref, k, pa, pb, core, rows):
        row = pl.multiple_of(pa * AROWS + pb * PROWS, PROWS)
        col = pl.multiple_of(core * (HD // 2) + k * CW, HSZ)
        return ref.at[:, pl.ds(row, rows), pl.ds(col, CW)]

    def scatter_copy(k, i):
        core, pa = rem(i, 2), lax.div(i, 2)
        src = piece(kv_hbm, k, pa, 0, core, AROWS)
        return remote(src, stage.at[k], sc_send.at[k, i], sc_recv.at[k], place(pa, 0, 0, core))

    def root_own(k):
        return pltpu.make_async_copy(piece(kv_hbm, k, 0, 0, 0, AROWS), stage.at[k], own_sem.at[k])

    @pl.when(is_root)
    def _():
        for k in range(NCH):
            root_own(k).start()
            for i in (4, 5, 2, 3, 6, 7, 1):
                scatter_copy(k, jnp.int32(i)).start()

    def sb_copy(k, d):
        src = stage.at[k, :, pl.ds(d * PROWS, PROWS), :]
        return remote(src, piece(anc, k, ca, rem(cb + d, NX), c, PROWS), sb_send.at[k, d - 1], sb_recv.at[k], bdev(d))

    def zb_copy(k, d):
        ref = piece(anc, k, ca, cb, c, PROWS)
        return remote(ref, ref, zb_send.at[k, d - 1], zb_recv.at[k], zdev(d))

    def bb_copy(k, pb, d):
        ref = piece(anc, k, ca, pb, c, PROWS)
        return remote(ref, ref, bb_send.at[k, d - 1], bb_recv.at[k, d - 1], bdev(d))

    def ab_copy(k, pa, d):
        ref = piece(anc, k, pa, 0, c, AROWS)
        return remote(ref, ref, ab_send.at[k, d - 1], ab_recv.at[k, d - 1], adev(d))

    def sib_copy(k, core):
        ref = piece(anc, k, 0, 0, core, BLK)
        return remote(ref, ref, sib_send.at[k], sib_recv.at[k], sibling)

    def anchor_first(k):
        @pl.when((z == 0) & (cb == 0))
        def _():
            @pl.when(is_root)
            def _():
                root_own(k).wait()

            @pl.when(jnp.logical_not(is_root))
            def _():
                remote(stage.at[k], stage.at[k], sib_send.at[k], sc_recv.at[k], sibling).wait_recv()

            for d in (2, 1, 3):
                sb_copy(k, d).start()
            row = pl.multiple_of(ca * AROWS, AROWS)
            col = pl.multiple_of(c * (HD // 2) + k * CW, HSZ)
            anc[:, pl.ds(row, PROWS), pl.ds(col, CW)] = stage[k, :, 0:PROWS, :]

    def anchor_second(k):
        @pl.when(z == 0)
        def _():
            @pl.when(cb > 0)
            def _():
                ref = piece(anc, k, ca, cb, c, PROWS)
                remote(ref, ref, sib_send.at[k], sb_recv.at[k], sibling).wait_recv()

            for d in (4, 3, 5, 2, 6, 1, 7):
                zb_copy(k, d).start()

    def anchor_z(k):
        @pl.when(z > 0)
        def _():
            zb_copy(k, 1).wait_recv()

        for d in (2, 1, 3):
            bb_copy(k, cb, d).start()

    def anchor_b(k):
        for d in range(1, NX):
            bb_copy(k, rem(cb + NX - d, NX), d).wait_recv()
        for d in (2, 1, 3):
            ab_copy(k, ca, d).start()

    def anchor_a(k):
        for d in range(1, NX):
            ab_copy(k, rem(ca + NX - d, NX), d).wait_recv()
        sib_copy(k, c).start()

    for copy in loads[3:]:
        copy.wait()
    flat = lax.broadcasted_iota(jnp.int32, (4, HSZ), 0) * HSZ + lax.broadcasted_iota(jnp.int32, (4, HSZ), 1)

    def key_bias(i, b, length, on):
        both = tok_v[i]
        ids = jnp.where(rem(b, 2) == 1, both[4:8], both[0:4])
        part = jnp.where((ids >= NAMB) & (flat < length) & on, 0.0, NEG)
        return jnp.concatenate([part[r : r + 1] for r in range(4)], axis=1)

    own_len = lens[block]
    own_bias = key_bias(0, block, own_len, True)
    bias[:, 0:BLK] = own_bias
    bias[:, BLK:] = key_bias(1, sblock, lens[sblock], True)
    abias[...] = key_bias(2, jnp.int32(0), lens[0], block > 0)
    row2d = lax.broadcasted_iota(jnp.int32, (BLK, BLK), 0)
    col2d = lax.broadcasted_iota(jnp.int32, (BLK, BLK), 1)
    own2d[...] = jnp.where(col2d == row2d, 0.0, jnp.where(col2d < row2d, own_bias, NEG))
    ksuf[:, 2 * SHARE :, :] = jnp.zeros((2, HSZ - 2 * SHARE, GH * HSZ), ksuf.dtype)

    def columns(h):
        return pl.ds(pl.multiple_of(h * HSZ, HSZ), HSZ)

    def wide(a, copies):
        return jnp.concatenate([a] * copies, axis=1)

    def pipelined(units, scores, finish):
        ready = scores(*units[0])
        for i, unit in enumerate(units):
            later = scores(*units[i + 1]) if i + 1 < len(units) else None
            finish(*unit, ready)
            ready = later

    loads[0].wait()
    loads[1].wait()

    def own_scores(h, t):
        q = q_v[t * TQ : (t + 1) * TQ, columns(h)]
        k = kv_v[0, 0 : (t + 1) * TQ, columns(h)]
        s = lax.dot_general(q, k, NT, preferred_element_type=jnp.float32)
        return s + own2d[t * TQ : (t + 1) * TQ, 0 : (t + 1) * TQ]

    def own_finish(h, t, s):
        rows = slice(t * TQ, (t + 1) * TQ)
        m = jnp.max(s, axis=1, keepdims=True)
        p = jnp.exp2((s - m) * SCALE2)
        v = kv_v[1, 0 : (t + 1) * TQ, columns(h)]
        l1[h, rows, :] = jnp.broadcast_to(jnp.sum(p, axis=1, keepdims=True), (TQ, HSZ))
        m1[h, rows, :] = jnp.broadcast_to(m, (TQ, HSZ))
        acc1[h, rows, :] = jnp.dot(p.astype(jnp.bfloat16), v, preferred_element_type=jnp.float32)

    @pl.loop(0, HEADS // 2)
    def _(t):
        pipelined([(2 * t + i, tile) for i in range(2) for tile in range(BLK // TQ)], own_scores, own_finish)

    def bq_copy(pb, d):
        ref = qbuf.at[ca, pb]
        return remote(ref, ref, bq_send.at[d - 1], bq_recv.at[d - 1], bdev(d))

    def aq_copy(pa, pb, d):
        ref = qbuf.at[pa, pb]
        return remote(ref, ref, aq_send.at[d - 1, pb], aq_recv.at[d - 1, pb], adev(d))

    for copy in zq:
        copy.wait_recv()
    for d in (2, 1, 3):
        bq_copy(cb, d).start()
    for d in (2, 1, 3):
        aq_copy(ca, cb, d).start()
    anchor_first(0)
    anchor_first(1)

    sk_copy.wait_recv()
    loads[2].wait()
    lane = lax.broadcasted_iota(jnp.int32, (QB, HSZ), 1)
    pair_lane = lax.broadcasted_iota(jnp.int32, (2 * QB, HSZ), 1)
    pair_row = lax.broadcasted_iota(jnp.int32, (2 * QB, HSZ), 0)

    def encode(o):
        a = jnp.maximum(jnp.max(jnp.abs(o), axis=-1, keepdims=True), 1e-30)
        return a, jnp.round(o * (CODE / a)).astype(jnp.int32).astype(jnp.int16)

    def suffix_pair(blocks, with_suffix):
        bx = jnp.where(first, *blocks[0])
        bys = [jnp.where(first, ib, ia) for ia, ib in blocks]

        def scores(e):
            q = jnp.concatenate([qbuf[ia, ib, e] for ia, ib in blocks], axis=0)
            parts = []
            for i, ref in enumerate((kv_v, kvs)):
                s = lax.dot_general(q, ref[0, :, columns(GH * bx + e)], NT, preferred_element_type=jnp.float32)
                parts.append(s + bias[:, i * BLK : (i + 1) * BLK])
            if with_suffix:
                by = jnp.where(pair_row < QB, bys[0], bys[1] - 1)
                qpos = by * (2 * QB) + lax.div(pair_row, SHARE) * (2 * SHARE) + c * SHARE + rem(pair_row, SHARE)
                other = (hst + 1 - 2 * c) * SHARE + pair_lane - SHARE
                kpos = jnp.where(pair_lane < SHARE, hst * SHARE + pair_lane, other)
                s = lax.dot_general(q, ksuf[0, :, e * HSZ : (e + 1) * HSZ], NT, preferred_element_type=jnp.float32)
                parts.append(jnp.where((pair_lane < 2 * SHARE) & (kpos <= qpos), s, NEG))
            return jnp.concatenate(parts, axis=1)

        columns_of = []

        def finish(e, s):
            m = jnp.maximum(jnp.max(s, axis=1, keepdims=True), FLOOR)
            p = jnp.exp2((s - m) * SCALE2)
            l = jnp.maximum(jnp.sum(p, axis=1, keepdims=True), 1.0)
            w = p.astype(jnp.bfloat16)
            h = GH * bx + e
            o = jnp.dot(w[:, :BLK], kv_v[1, :, columns(h)], preferred_element_type=jnp.float32)
            o = o + jnp.dot(w[:, BLK : 2 * BLK], kvs[1, :, columns(h)], preferred_element_type=jnp.float32)
            if with_suffix:
                v = ksuf[1, :, e * HSZ : (e + 1) * HSZ]
                o = o + jnp.dot(w[:, 2 * BLK :], v, preferred_element_type=jnp.float32)
            a, code = encode(o / l)
            lse = m * SCALE2 + jnp.log2(l)
            for i, (ia, ib) in enumerate(blocks):
                codes[ia, ib, e] = code[i * QB : (i + 1) * QB]
            columns_of.append((lse, a))

        pipelined([(e,) for e in range(GH)], scores, finish)
        for i, (ia, ib) in enumerate(blocks):
            rows = slice(i * QB, (i + 1) * QB)
            stats[ia, ib] = rows_of([(lse[rows], a[rows]) for lse, a in columns_of])

    def rows_of(columns_of):
        flat_stats = jnp.zeros((QB, HSZ), jnp.float32)
        for e, (lse, a) in enumerate(columns_of):
            flat_stats = jnp.where(lane == e, lse, jnp.where(lane == 4 + e, a, flat_stats))
        return flat_stats.T[0:8]

    def merge(parts):
        lses = [s[0:4] for s in parts]
        top = lses[0]
        for s in lses[1:]:
            top = jnp.maximum(top, s)
        weights = [jnp.exp2(s - top) for s in lses]
        total = weights[0]
        for w in weights[1:]:
            total = total + w
        inverse = 1.0 / (total * CODE)
        rows = jnp.concatenate([w * inverse * s[4:8] for w, s in zip(weights, parts)], axis=0)
        rows = jnp.concatenate([rows, jnp.zeros((HSZ - rows.shape[0], HSZ), jnp.float32)], axis=0)
        return rows.T, top + jnp.log2(total)

    def blend(coefficients, coded, e):
        total = None
        for i, code in enumerate(coded):
            term = coefficients[:, 4 * i + e : 4 * i + e + 1] * code.astype(jnp.int32).astype(jnp.float32)
            total = term if total is None else total + term
        return total

    def blend_and_encode(parts, coded_of, store):
        coefficients, lse = merge(parts)
        scales = []
        for e in range(GH):
            a, code = encode(blend(coefficients, coded_of(e), e))
            store(e, code)
            scales.append((a, a))
        return jnp.concatenate([lse, rows_of(scales)[0:4]], axis=0)

    def rb_copies(ia, d):
        ib = rem(cb + d, NX)
        return [
            remote(codes.at[ia, ib], rb.at[d - 1, ia], rb_send.at[0, d - 1, ia], rb_recv.at[0, d - 1, ia], bdev(d)),
            remote(stats.at[ia, ib], rbs.at[d - 1, ia], rb_send.at[1, d - 1, ia], rb_recv.at[1, d - 1, ia], bdev(d)),
        ]

    def ra_copies(d):
        ia = rem(ca + d, NX)
        return [
            remote(codes2.at[ia], ra.at[d - 1], ra_send.at[0, d - 1], ra_recv.at[0, d - 1], adev(d)),
            remote(stats2.at[ia], ras.at[d - 1], ra_send.at[1, d - 1], ra_recv.at[1, d - 1], adev(d)),
        ]

    def rz_copies(d):
        rows = pl.ds(pl.multiple_of(rem(z + d, NZ) * SHARE, SHARE), SHARE)
        return [
            remote(codes3.at[:, rows, :], rz.at[d - 1], rz_send.at[0, d - 1], rz_recv.at[0, d - 1], zdev(d)),
            remote(stats3, rzs.at[d - 1], rz_send.at[1, d - 1], rz_recv.at[1, d - 1], zdev(d)),
        ]

    def reduce_b(delta):
        ia = rem(ca + delta, NX)
        for d in range(1, NX):
            for copy in rb_copies(ia, d):
                copy.wait_recv()

        def store(e, code):
            codes2[ia, e] = code

        stats2[ia] = blend_and_encode(
            [stats[ia, cb]] + [rbs[d, ia] for d in range(NX - 1)],
            lambda e: [codes[ia, cb, e]] + [rb[d, ia, e] for d in range(NX - 1)],
            store,
        )
        if delta:
            for copy in ra_copies(delta):
                copy.start()

    def reduce_a():
        for d in range(1, NX):
            for copy in ra_copies(d):
                copy.wait_recv()

        def store(e, code):
            codes3[e] = code

        stats3[...] = blend_and_encode(
            [stats2[ca]] + [ras[d] for d in range(NX - 1)],
            lambda e: [codes2[ca, e]] + [ra[d, e] for d in range(NX - 1)],
            store,
        )
        for d in (4, 3, 5, 2, 6, 1, 7):
            for copy in rz_copies(d):
                copy.start()

    def reduce_z():
        for d in range(1, NZ):
            for copy in rz_copies(d):
                copy.wait_recv()
        turned[...], unused = merge([stats3[...]] + [rzs[d] for d in range(NZ - 1)])
        rows = pl.ds(zrow, SHARE)
        coefficients = turned[rows, :]
        for e in range(GH):
            o = blend(coefficients, [codes3[e, rows, :]] + [rz[d, e] for d in range(NZ - 1)], e)
            suf_ref[:, e * HSZ : (e + 1) * HSZ] = o.astype(suf_ref.dtype)

    def q_b():
        for d in range(1, NX):
            bq_copy(rem(cb + NX - d, NX), d).wait_recv()
        for i in range(1, NX):
            for d in (2, 1, 3):
                aq_copy(ca, rem(cb + i, NX), d).start()

    def all_of(*steps):
        def run():
            for step, *arguments in steps:
                step(*arguments)

        return run

    q_b()
    kvs_copy.wait_recv()
    anchor_first(2)
    anchor_second(0)

    before = {
        1: all_of((anchor_second, 1)),
        2: all_of((anchor_second, 2)),
        4: all_of((anchor_z, 0)),
        5: all_of((anchor_z, 1)),
        6: all_of((anchor_b, 0)),
        7: all_of((anchor_z, 2)),
    }

    @pl.loop(0, NX * NY // 2)
    def _(n):
        for at, event in before.items():
            pl.when(n == at)(event)
        group, step, late = lax.div(n, 2), 2 * rem(n, 2), jnp.where(n < 4, 0, 3)
        delta = jnp.where(group < 2, group, 5 - group)
        deltas = (jnp.where(first, delta, late), jnp.where(first, delta, jnp.where(n < 4, 1, 2)))
        steps = (jnp.where(first, step, rem(n, 4)), jnp.where(first, step + 1, rem(n, 4)))
        blocks = [(rem(ca + delta, NX), rem(cb + step, NX)) for delta, step in zip(deltas, steps)]
        for delta, (ia, ib) in zip(deltas, blocks):

            @pl.when(delta > 0)
            def _():
                aq_copy(ia, ib, jnp.where(delta > 0, NX - delta, 1)).wait_recv()

        own_heads = jnp.where(first, *blocks[0]) == x

        @pl.when(own_heads)
        def _():
            suffix_pair(blocks, True)

        @pl.when(jnp.logical_not(own_heads))
        def _():
            suffix_pair(blocks, False)

        for step, (ia, ib) in zip(steps, blocks):

            @pl.when(step > 0)
            def _():
                for copy in rb_copies(ia, jnp.where(step > 0, step, 1)):
                    copy.start()

    anchor_b(1)
    reduce_b(1)
    reduce_b(3)
    anchor_b(2)
    anchor_a(0)
    reduce_b(2)

    def anchor_scores(h, t):
        q = q_v[t * TQ : (t + 1) * TQ, columns(h)]
        return lax.dot_general(q, anc[0, :, columns(h)], NT, preferred_element_type=jnp.float32) + abias[...]

    def anchor_finish(h, t, s):
        rows = slice(t * TQ, (t + 1) * TQ)
        before = m1[h, rows, :]
        m = jnp.maximum(before, jnp.max(s, axis=1, keepdims=True))
        p = jnp.exp2((s - wide(m, BLK // HSZ)) * SCALE2)
        fade = jnp.exp2((before - m) * SCALE2)
        l = l1[h, rows, :] * fade + jnp.sum(p, axis=1, keepdims=True)
        o = jnp.dot(p.astype(jnp.bfloat16), anc[1, :, columns(h)], preferred_element_type=jnp.float32)
        o = (acc1[h, rows, :] * fade + o) / l
        token = lax.broadcasted_iota(jnp.int32, (TQ, HSZ), 0) + t * TQ
        obuf[h, rows, :] = jnp.where(token < own_len, o, 0.0).astype(obuf.dtype)

    def out_copy(h):
        return pltpu.make_async_copy(obuf.at[h], ctx_hbm.at[:, columns(h)], out_sem.at[h])

    tail = {
        1: all_of((anchor_a, 1)),
        2: all_of((anchor_a, 2), (reduce_b, 0)),
        4: all_of((reduce_a,)),
    }

    @pl.loop(0, HEADS // 2)
    def _(t):
        for at, event in tail.items():
            pl.when(t == at)(event)
        k, other = lax.div(t, 2), rem(t, 2)

        @pl.when(other == 1)
        def _():
            sib_copy(k, 1 - c).wait_recv()

        h = rem(c + other, 2) * (HEADS // 2) + 2 * k
        pipelined([(h + i, tile) for i in range(2) for tile in range(BLK // TQ)], anchor_scores, anchor_finish)
        for i in range(2):
            out_copy(h + i).start()

    reduce_z()

    for copy in zq + [kvs_copy, sk_copy]:
        copy.wait_send()
    for d in range(1, NX):
        bq_copy(cb, d).wait_send()
        for pb in range(NX):
            aq_copy(ca, pb, d).wait_send()
        for copy in ra_copies(d):
            copy.wait_send()

    @pl.loop(0, NX)
    def _(ia):
        for d in range(1, NX):
            for copy in rb_copies(ia, d):
                copy.wait_send()

    @pl.loop(0, NCH)
    def _(k):
        for d in range(1, NX):
            bb_copy(k, cb, d).wait_send()
            ab_copy(k, ca, d).wait_send()
        sib_copy(k, c).wait_send()

        @pl.when(z == 0)
        def _():
            for d in range(1, NZ):
                zb_copy(k, d).wait_send()

        @pl.when((z == 0) & (cb == 0))
        def _():
            for d in range(1, NX):
                sb_copy(k, d).wait_send()

        @pl.when(is_root)
        def _():
            @pl.loop(1, 2 * NX)
            def _(i):
                scatter_copy(k, i).wait_send()

    for d in range(1, NZ):
        for copy in rz_copies(d):
            copy.wait_send()

    @pl.loop(0, HEADS)
    def _(h):
        out_copy(h).wait()


def per_device(queries, keys_values, token_ids, lengths, suffix_queries, suffix_kv):
    bf16, f32, i16 = jnp.bfloat16, jnp.float32, jnp.int16
    dma = pltpu.SemaphoreType.DMA
    scratch = [
        pltpu.VMEM((BLK, HD), bf16),
        pltpu.VMEM((2, BLK, HD), bf16),
        pltpu.VMEM((2, BLK, HD), bf16),
        pltpu.VMEM((3, 8, HSZ), jnp.int32),
        pltpu.VMEM((2, HSZ, GH * HSZ), bf16),
        pltpu.VMEM((NX, NX, GH, QB, HSZ), bf16),
        pltpu.VMEM((2, BLK, HD), bf16),
        pltpu.VMEM((NCH, 2, AROWS, CW), bf16),
        pltpu.VMEM((HEADS, BLK, HSZ), f32),
        pltpu.VMEM((HEADS, BLK, HSZ), f32),
        pltpu.VMEM((HEADS, BLK, HSZ), f32),
        pltpu.VMEM((BLK, BLK), f32),
        pltpu.VMEM((1, 2 * BLK), f32),
        pltpu.VMEM((1, BLK), f32),
        pltpu.VMEM((NX, NX, GH, QB, HSZ), i16),
        pltpu.VMEM((NX, NX, 8, HSZ), f32),
        pltpu.VMEM((NX - 1, NX, GH, QB, HSZ), i16),
        pltpu.VMEM((NX - 1, NX, 8, HSZ), f32),
        pltpu.VMEM((NX, GH, QB, HSZ), i16),
        pltpu.VMEM((NX, 8, HSZ), f32),
        pltpu.VMEM((NX - 1, GH, QB, HSZ), i16),
        pltpu.VMEM((NX - 1, 8, HSZ), f32),
        pltpu.VMEM((GH, QB, HSZ), i16),
        pltpu.VMEM((8, HSZ), f32),
        pltpu.VMEM((NZ - 1, GH, SHARE, HSZ), i16),
        pltpu.VMEM((NZ - 1, 8, HSZ), f32),
        pltpu.VMEM((HSZ, HSZ), f32),
        pltpu.VMEM((HEADS, BLK, HSZ), bf16),
        dma((9,)),
        dma, dma, dma, dma,
        dma((NZ - 1,)), dma((NZ - 1,)),
        dma((NX - 1,)), dma((NX - 1,)),
        dma((NX - 1, NX)), dma((NX - 1, NX)),
        dma((NCH, 2 * NX)), dma((NCH,)), dma((NCH,)),
        dma((NCH, NX - 1)), dma((NCH,)),
        dma((NCH, NZ - 1)), dma((NCH,)),
        dma((NCH, NX - 1)), dma((NCH, NX - 1)),
        dma((NCH, NX - 1)), dma((NCH, NX - 1)),
        dma((NCH,)), dma((NCH,)),
        dma((2, NX - 1, NX)), dma((2, NX - 1, NX)),
        dma((2, NX - 1)), dma((2, NX - 1)),
        dma((2, NZ - 1)), dma((2, NZ - 1)),
        dma((HEADS,)),
    ]
    anywhere = pl.BlockSpec(memory_space=pl.ANY)
    return pl.pallas_call(
        kernel,
        out_shape=(
            jax.ShapeDtypeStruct((BLK, HD), bf16),
            jax.ShapeDtypeStruct((SHARE, GH * HSZ), bf16),
        ),
        in_specs=[anywhere, anywhere, anywhere, pl.BlockSpec(memory_space=pltpu.SMEM), anywhere, anywhere],
        out_specs=(anywhere, pl.BlockSpec(memory_space=pltpu.VMEM)),
        scratch_shapes=scratch,
        compiler_params=pltpu.CompilerParams(
            collective_id=0, has_side_effects=True, vmem_limit_bytes=56 * 2**20
        ),
        cost_estimate=pl.CostEstimate(
            flops=6_500_000_000, bytes_accessed=6_500_000, transcendentals=12_600_000
        ),
        name="star",
    )(queries, keys_values, token_ids.reshape(-1, HSZ), lengths, suffix_queries, suffix_kv)


def solution(mesh):
    return jax.shard_map(
        per_device,
        mesh=mesh,
        in_specs=(
            P(("hst", "grp"), None),
            P(None, ("hst", "grp"), None),
            P(),
            P(),
            P("hst", "grp"),
            P(None, "hst", "grp"),
        ),
        out_specs=(P(("hst", "grp"), None), P("hst", "grp")),
        check_vma=False,
    )
```

time: 910 us -> 73.1 us (0.08)
  blocking collectives: 551 us -> 0 us
  waiting for transfers between devices: 201 us -> 0 us
  Pallas kernels: 0 us -> 69.1 us
  matrix products: 56.6 us -> 0 us
  other arithmetic: 38.7 us -> 0 us
  local copies, waits for them, and re-layouts: 34.2 us -> 3.26 us
  between operations: 15.7 us -> 0.65 us
    pmax x1 -> x0, blocking collectives: 247 us -> none  [per_device(): upper = lax.pmax(tops, 'hst')]
    psum x1 -> x0, blocking collectives: 246 us -> none  [per_device(): acc, summed = lax.psum((scaled_parts, scaled_totals), 'hst')]
    psum x2 -> x0, waiting for transfers between devices: 201 us -> none  [the longest x1 201 us: broadcast(): return lax.psum(block, axis)]
    pallas_call x0 -> x1, Pallas kernels: none -> 69.1 us  [per_device(): pl.pallas_call(kernel, out_shape=(jax.ShapeDtypeStruct((BLK, HD), bf16),...]
    all_gather x1 -> x0, blocking collectives: 57.4 us -> none  [per_device(): gathered = lax.all_gather(suffix_queries, 'hst', axis=0, tiled=True)]
    dot_general x5 -> x0, matrix products: 38.1 us -> none  [the longest x3 23 us: attend(): jnp.einsum('hqk,khd->qhd', weights.astype(jnp.bfloat16), values, preferre...]
    sub x1 -> x0, matrix products: 18.5 us -> none  [attend(): weights = jnp.where(valid[None], jnp.exp(masked - top[..., None]), 0.0)]
    unnamed x25 -> x4, local copies, waits for them, and re-layouts: 20.5 us -> 3.26 us
  transfers between devices with their start and end apart: 3 -> 0, of which waited for: 1 -> 0; matrix products, arithmetic and copies ran while one was open for 5% -> 0% of each run, Pallas kernels for 0% -> 0%
where the time goes in v2:
time: 73.1 us; the launch traced here: 73 us
  Pallas kernels  69.1 us (95%)
  local copies, waits for them, and re-layouts  3.26 us (4%)
    pallas_call x1, Pallas kernels, per_device(): pl.pallas_call(kernel, out_shape=(jax.ShapeDtypeStruct((BLK, HD), bf16),...  69.1 us
    unnamed x4, local copies, waits for them, and re-layouts  3.26 us

profile of v2, /device:TPU:32, one launch (start us, length us, event | category | flops | bytes accessed | tf_op | source)
XLA Modules:
  0.0 73.0 jit_solution(12336447616825311127)
XLA Ops:
  0.6 69.1 %star.1 = (bf16[512,1536]{1,0:T(8,128)(2,1)}, bf16[16,384]{1,0:T(8,128)(2,1)}) custom-call(bf16[512,1536]{1,0:T(8,128)(2,1)} %q_hbm.1, bf16[2,512,1536]{2,1,0:T(8,128)(2,1)} %kv_hbm.1, s32[1024,128]{1,0:T(8,128)} %bitcast.1, s32[256]{0:T(256)} %lens.1, bf16[16,384]{1,0:T(8,128)(2,1)} %sq_hbm.1, bf16[2,16,384]{2,1,0:T(8,128)(2,1)} %skv_hbm.1), custom_call_target="tpu_custom_call" | custom-call | flops 6499999744 | bytes 6500000 | tf_op jit(solution)/shard_map/star/pallas_call | solution.py:648
  69.7 0.0 copy-start
  69.7 2.7 %copy.10 = bf16[512,1536]{1,0:T(8,128)(2,1)} copy(bf16[512,1536]{1,0:T(8,128)(2,1)} %get-tuple-element.4) | data formatting | bytes 3145728
  72.4 0.0 copy-done
  72.4 0.6 copy.11
Async XLA Ops:
  69.7 2.7 %copy-start = (bf16[16,384]{1,0:T(8,128)(2,1)S(1)}, bf16[16,384]{1,0:T(8,128)(2,1)}, u32[]{:S(2)}) copy-start(bf16[16,384]{1,0:T(8,128)(2,1)} %get-tuple-element.5) | copy-start | bytes 36868

commit v3 on v2

--- a/solution.py
+++ b/solution.py
@@ -36,14 +36,14 @@
 
 def kernel(
     q_hbm, kv_hbm, tok_hbm, lens, sq_hbm, skv_hbm,
-    ctx_hbm, suf_ref,
+    ctx_out, suf_out,
     q_v, kv_v, kvs, tok_v, ksuf, qbuf, anc, stage, acc1, m1, l1, own2d, bias, abias,
-    codes, stats, rb, rbs, codes2, stats2, ra, ras, codes3, stats3, rz, rzs, turned, obuf,
+    codes, stats, rb, rbs, codes2, stats2, ra, ras, codes3, stats3, rz, rzs, turned, obuf, suf_v,
     in_sem, kvs_send, kvs_recv, sk_send, sk_recv,
     zq_send, zq_recv, bq_send, bq_recv, aq_send, aq_recv,
     sc_send, sc_recv, own_sem, sb_send, sb_recv, zb_send, zb_recv, bb_send, bb_recv, ab_send, ab_recv, sib_send, sib_recv,
     rb_send, rb_recv, ra_send, ra_recv, rz_send, rz_recv,
-    out_sem,
+    out_sem, suf_sem,
 ):
     hst = lax.axis_index("hst")
     x = lax.axis_index("grp")
@@ -78,11 +78,17 @@
             src_ref=src, dst_ref=dst, send_sem=send, recv_sem=recv, device_id=to, device_id_type=MESH
         )
 
+    def sent(ref, send):
+        remote(ref, ref, send, kvs_recv, sibling).wait_send()
+
+    def received(ref, recv):
+        remote(ref, ref, kvs_send, recv, sibling).wait_recv()
+
     sblock = (hst + 1 - 2 * c) * NX + x
     zrow = pl.multiple_of(z * SHARE, SHARE)
     qloads = [
         pltpu.make_async_copy(
-            sq_hbm.at[:, pl.ds(e * HSZ, HSZ)], qbuf.at[ca, cb, e, pl.ds(zrow, SHARE), :], in_sem.at[6 + e]
+            sq_hbm.at[:, pl.ds(e * HSZ, HSZ)], qbuf.at[ca, cb, e, pl.ds(zrow, SHARE), :], in_sem.at[4]
         )
         for e in range(GH)
     ]
@@ -93,7 +99,7 @@
     ]
     for i, b in enumerate((block, sblock, 0)):
         row = pl.multiple_of(lax.div(b, 2) * 8, 8)
-        loads.append(pltpu.make_async_copy(tok_hbm.at[pl.ds(row, 8), :], tok_v.at[i], in_sem.at[3 + i]))
+        loads.append(pltpu.make_async_copy(tok_hbm.at[pl.ds(row, 8), :], tok_v.at[pl.ds(8 * i, 8), :], in_sem.at[3]))
     for copy in qloads + loads:
         copy.start()
 
@@ -112,12 +118,12 @@
 
     pl.semaphore_wait(barrier, len(partners) + jnp.where(is_root, NY - 1, 0))
 
-    for copy in qloads:
-        copy.wait()
+    ref = qbuf.at[ca, cb, :, pl.ds(zrow, SHARE), :]
+    pltpu.make_async_copy(ref, ref, in_sem.at[4]).wait()
     zq = []
     for d in range(1, NZ):
         ref = qbuf.at[ca, cb, :, pl.ds(zrow, SHARE), :]
-        zq.append(remote(ref, ref, zq_send.at[d - 1], zq_recv.at[d - 1], zdev(d)))
+        zq.append(remote(ref, ref, zq_send, zq_recv, zdev(d)))
         zq[-1].start()
 
     kvs_copy = remote(kv_hbm, kvs, kvs_send, kvs_recv, sibling)
@@ -133,7 +139,7 @@
     def scatter_copy(k, i):
         core, pa = rem(i, 2), lax.div(i, 2)
         src = piece(kv_hbm, k, pa, 0, core, AROWS)
-        return remote(src, stage.at[k], sc_send.at[k, i], sc_recv.at[k], place(pa, 0, 0, core))
+        return remote(src, stage.at[k], sc_send, sc_recv.at[k], place(pa, 0, 0, core))
 
     def root_own(k):
         return pltpu.make_async_copy(piece(kv_hbm, k, 0, 0, 0, AROWS), stage.at[k], own_sem.at[k])
@@ -147,23 +153,23 @@
 
     def sb_copy(k, d):
         src = stage.at[k, :, pl.ds(d * PROWS, PROWS), :]
-        return remote(src, piece(anc, k, ca, rem(cb + d, NX), c, PROWS), sb_send.at[k, d - 1], sb_recv.at[k], bdev(d))
+        return remote(src, piece(anc, k, ca, rem(cb + d, NX), c, PROWS), sb_send, sb_recv.at[k], bdev(d))
 
     def zb_copy(k, d):
         ref = piece(anc, k, ca, cb, c, PROWS)
-        return remote(ref, ref, zb_send.at[k, d - 1], zb_recv.at[k], zdev(d))
+        return remote(ref, ref, zb_send, zb_recv.at[k], zdev(d))
 
     def bb_copy(k, pb, d):
         ref = piece(anc, k, ca, pb, c, PROWS)
-        return remote(ref, ref, bb_send.at[k, d - 1], bb_recv.at[k, d - 1], bdev(d))
+        return remote(ref, ref, bb_send, bb_recv.at[k], bdev(d))
 
     def ab_copy(k, pa, d):
         ref = piece(anc, k, pa, 0, c, AROWS)
-        return remote(ref, ref, ab_send.at[k, d - 1], ab_recv.at[k, d - 1], adev(d))
+        return remote(ref, ref, ab_send, ab_recv.at[k], adev(d))
 
     def sib_copy(k, core):
         ref = piece(anc, k, 0, 0, core, BLK)
-        return remote(ref, ref, sib_send.at[k], sib_recv.at[k], sibling)
+        return remote(ref, ref, sib_send, sib_recv.at[k], sibling)
 
     def anchor_first(k):
         @pl.when((z == 0) & (cb == 0))
@@ -174,7 +180,7 @@
 
             @pl.when(jnp.logical_not(is_root))
             def _():
-                remote(stage.at[k], stage.at[k], sib_send.at[k], sc_recv.at[k], sibling).wait_recv()
+                remote(stage.at[k], stage.at[k], sib_send, sc_recv.at[k], sibling).wait_recv()
 
             for d in (2, 1, 3):
                 sb_copy(k, d).start()
@@ -188,7 +194,7 @@
             @pl.when(cb > 0)
             def _():
                 ref = piece(anc, k, ca, cb, c, PROWS)
-                remote(ref, ref, sib_send.at[k], sb_recv.at[k], sibling).wait_recv()
+                remote(ref, ref, sib_send, sb_recv.at[k], sibling).wait_recv()
 
             for d in (4, 3, 5, 2, 6, 1, 7):
                 zb_copy(k, d).start()
@@ -202,22 +208,19 @@
             bb_copy(k, cb, d).start()
 
     def anchor_b(k):
-        for d in range(1, NX):
-            bb_copy(k, rem(cb + NX - d, NX), d).wait_recv()
+        received(anc.at[:, pl.ds(0, (NX - 1) * PROWS), pl.ds(0, CW)], bb_recv.at[k])
         for d in (2, 1, 3):
             ab_copy(k, ca, d).start()
 
     def anchor_a(k):
-        for d in range(1, NX):
-            ab_copy(k, rem(ca + NX - d, NX), d).wait_recv()
+        received(anc.at[:, pl.ds(0, (NX - 1) * AROWS), pl.ds(0, CW)], ab_recv.at[k])
         sib_copy(k, c).start()
 
-    for copy in loads[3:]:
-        copy.wait()
+    pltpu.make_async_copy(tok_hbm.at[pl.ds(0, 24), :], tok_v, in_sem.at[3]).wait()
     flat = lax.broadcasted_iota(jnp.int32, (4, HSZ), 0) * HSZ + lax.broadcasted_iota(jnp.int32, (4, HSZ), 1)
 
     def key_bias(i, b, length, on):
-        both = tok_v[i]
+        both = tok_v[8 * i : 8 * i + 8]
         ids = jnp.where(rem(b, 2) == 1, both[4:8], both[0:4])
         part = jnp.where((ids >= NAMB) & (flat < length) & on, 0.0, NEG)
         return jnp.concatenate([part[r : r + 1] for r in range(4)], axis=1)
@@ -269,14 +272,13 @@
 
     def bq_copy(pb, d):
         ref = qbuf.at[ca, pb]
-        return remote(ref, ref, bq_send.at[d - 1], bq_recv.at[d - 1], bdev(d))
+        return remote(ref, ref, bq_send, bq_recv, bdev(d))
 
     def aq_copy(pa, pb, d):
         ref = qbuf.at[pa, pb]
-        return remote(ref, ref, aq_send.at[d - 1, pb], aq_recv.at[d - 1, pb], adev(d))
-
-    for copy in zq:
-        copy.wait_recv()
+        return remote(ref, ref, aq_send, aq_recv.at[d - 1, pb], adev(d))
+
+    received(qbuf.at[0, 0, :, pl.ds(0, (NZ - 1) * SHARE), :], zq_recv)
     for d in (2, 1, 3):
         bq_copy(cb, d).start()
     for d in (2, 1, 3):
@@ -376,29 +378,28 @@
     def rb_copies(ia, d):
         ib = rem(cb + d, NX)
         return [
-            remote(codes.at[ia, ib], rb.at[d - 1, ia], rb_send.at[0, d - 1, ia], rb_recv.at[0, d - 1, ia], bdev(d)),
-            remote(stats.at[ia, ib], rbs.at[d - 1, ia], rb_send.at[1, d - 1, ia], rb_recv.at[1, d - 1, ia], bdev(d)),
+            remote(codes.at[ia, ib], rb.at[d - 1, ia], rb_send.at[0], rb_recv.at[0, ia], bdev(d)),
+            remote(stats.at[ia, ib], rbs.at[d - 1, ia], rb_send.at[1], rb_recv.at[1, ia], bdev(d)),
         ]
 
     def ra_copies(d):
         ia = rem(ca + d, NX)
         return [
-            remote(codes2.at[ia], ra.at[d - 1], ra_send.at[0, d - 1], ra_recv.at[0, d - 1], adev(d)),
-            remote(stats2.at[ia], ras.at[d - 1], ra_send.at[1, d - 1], ra_recv.at[1, d - 1], adev(d)),
+            remote(codes2.at[ia], ra.at[d - 1], ra_send.at[0], ra_recv.at[0], adev(d)),
+            remote(stats2.at[ia], ras.at[d - 1], ra_send.at[1], ra_recv.at[1], adev(d)),
         ]
 
     def rz_copies(d):
         rows = pl.ds(pl.multiple_of(rem(z + d, NZ) * SHARE, SHARE), SHARE)
         return [
-            remote(codes3.at[:, rows, :], rz.at[d - 1], rz_send.at[0, d - 1], rz_recv.at[0, d - 1], zdev(d)),
-            remote(stats3, rzs.at[d - 1], rz_send.at[1, d - 1], rz_recv.at[1, d - 1], zdev(d)),
+            remote(codes3.at[:, rows, :], rz.at[d - 1], rz_send.at[0], rz_recv.at[0], zdev(d)),
+            remote(stats3, rzs.at[d - 1], rz_send.at[1], rz_recv.at[1], zdev(d)),
         ]
 
     def reduce_b(delta):
         ia = rem(ca + delta, NX)
-        for d in range(1, NX):
-            for copy in rb_copies(ia, d):
-                copy.wait_recv()
+        received(rb.at[:, ia], rb_recv.at[0, ia])
+        received(rbs.at[:, ia], rb_recv.at[1, ia])
 
         def store(e, code):
             codes2[ia, e] = code
@@ -413,9 +414,8 @@
                 copy.start()
 
     def reduce_a():
-        for d in range(1, NX):
-            for copy in ra_copies(d):
-                copy.wait_recv()
+        received(ra, ra_recv.at[0])
+        received(ras, ra_recv.at[1])
 
         def store(e, code):
             codes3[e] = code
@@ -430,19 +430,18 @@
                 copy.start()
 
     def reduce_z():
-        for d in range(1, NZ):
-            for copy in rz_copies(d):
-                copy.wait_recv()
+        received(rz, rz_recv.at[0])
+        received(rzs, rz_recv.at[1])
         turned[...], unused = merge([stats3[...]] + [rzs[d] for d in range(NZ - 1)])
         rows = pl.ds(zrow, SHARE)
         coefficients = turned[rows, :]
         for e in range(GH):
             o = blend(coefficients, [codes3[e, rows, :]] + [rz[d, e] for d in range(NZ - 1)], e)
-            suf_ref[:, e * HSZ : (e + 1) * HSZ] = o.astype(suf_ref.dtype)
+            suf_v[:, e * HSZ : (e + 1) * HSZ] = o.astype(suf_v.dtype)
+        pltpu.make_async_copy(suf_v, suf_out, suf_sem).start()
 
     def q_b():
-        for d in range(1, NX):
-            bq_copy(rem(cb + NX - d, NX), d).wait_recv()
+        received(qbuf.at[0, pl.ds(0, NX - 1)], bq_recv)
         for i in range(1, NX):
             for d in (2, 1, 3):
                 aq_copy(ca, rem(cb + i, NX), d).start()
@@ -460,12 +459,13 @@
     anchor_second(0)
 
     before = {
-        1: all_of((anchor_second, 1)),
-        2: all_of((anchor_second, 2)),
-        4: all_of((anchor_z, 0)),
-        5: all_of((anchor_z, 1)),
-        6: all_of((anchor_b, 0)),
-        7: all_of((anchor_z, 2)),
+        0: all_of((anchor_second, 1)),
+        1: all_of((anchor_second, 2)),
+        3: all_of((anchor_z, 0)),
+        4: all_of((anchor_z, 1)),
+        5: all_of((anchor_z, 2), (anchor_b, 0)),
+        6: all_of((anchor_b, 1)),
+        7: all_of((anchor_b, 2), (reduce_b, 1)),
     }
 
     @pl.loop(0, NX * NY // 2)
@@ -500,12 +500,9 @@
                 for copy in rb_copies(ia, jnp.where(step > 0, step, 1)):
                     copy.start()
 
-    anchor_b(1)
-    reduce_b(1)
+    anchor_a(0)
+    reduce_b(0)
     reduce_b(3)
-    anchor_b(2)
-    anchor_a(0)
-    reduce_b(2)
 
     def anchor_scores(h, t):
         q = q_v[t * TQ : (t + 1) * TQ, columns(h)]
@@ -524,11 +521,11 @@
         obuf[h, rows, :] = jnp.where(token < own_len, o, 0.0).astype(obuf.dtype)
 
     def out_copy(h):
-        return pltpu.make_async_copy(obuf.at[h], ctx_hbm.at[:, columns(h)], out_sem.at[h])
+        return pltpu.make_async_copy(obuf.at[h], ctx_out.at[:, columns(h)], out_sem)
 
     tail = {
-        1: all_of((anchor_a, 1)),
-        2: all_of((anchor_a, 2), (reduce_b, 0)),
+        1: all_of((anchor_a, 1), (reduce_b, 2)),
+        2: all_of((anchor_a, 2)),
         4: all_of((reduce_a,)),
     }
 
@@ -549,51 +546,36 @@
 
     reduce_z()
 
-    for copy in zq + [kvs_copy, sk_copy]:
+    for copy in (kvs_copy, sk_copy):
         copy.wait_send()
-    for d in range(1, NX):
-        bq_copy(cb, d).wait_send()
-        for pb in range(NX):
-            aq_copy(ca, pb, d).wait_send()
-        for copy in ra_copies(d):
-            copy.wait_send()
-
-    @pl.loop(0, NX)
-    def _(ia):
-        for d in range(1, NX):
-            for copy in rb_copies(ia, d):
-                copy.wait_send()
-
-    @pl.loop(0, NCH)
-    def _(k):
-        for d in range(1, NX):
-            bb_copy(k, cb, d).wait_send()
-            ab_copy(k, ca, d).wait_send()
-        sib_copy(k, c).wait_send()
-
-        @pl.when(z == 0)
+    sent(qbuf.at[0, 0, :, pl.ds(0, (NZ - 1) * SHARE), :], zq_send)
+    sent(qbuf.at[0, pl.ds(0, NX - 1)], bq_send)
+    sent(qbuf.at[pl.ds(0, NX - 1)], aq_send)
+    sent(codes.at[pl.ds(0, NX - 1)], rb_send.at[0])
+    sent(stats.at[pl.ds(0, NX - 1)], rb_send.at[1])
+    sent(ra, ra_send.at[0])
+    sent(ras, ra_send.at[1])
+    sent(rz, rz_send.at[0])
+    sent(rzs, rz_send.at[1])
+    half = pl.ds(0, HD // 2)
+    sent(anc.at[:, pl.ds(0, (NX - 1) * PROWS), half], bb_send)
+    sent(anc.at[:, pl.ds(0, (NX - 1) * AROWS), half], ab_send)
+    sent(anc.at[:, :, half], sib_send)
+
+    @pl.when(z == 0)
+    def _():
+        sent(anc.at[:, pl.ds(0, (NZ - 1) * PROWS // 2), :], zb_send)
+
+        @pl.when(cb == 0)
         def _():
-            for d in range(1, NZ):
-                zb_copy(k, d).wait_send()
-
-        @pl.when((z == 0) & (cb == 0))
-        def _():
-            for d in range(1, NX):
-                sb_copy(k, d).wait_send()
-
-        @pl.when(is_root)
-        def _():
-            @pl.loop(1, 2 * NX)
-            def _(i):
-                scatter_copy(k, i).wait_send()
-
-    for d in range(1, NZ):
-        for copy in rz_copies(d):
-            copy.wait_send()
-
-    @pl.loop(0, HEADS)
-    def _(h):
-        out_copy(h).wait()
+            sent(anc.at[:, pl.ds(0, (NX - 1) * PROWS), half], sb_send)
+
+    @pl.when(is_root)
+    def _():
+        sent(kv_v.at[:, pl.ds(0, (2 * NX - 1) * AROWS // 2), :], sc_send)
+
+    pltpu.make_async_copy(suf_v, suf_out, suf_sem).wait()
+    pltpu.make_async_copy(q_v, ctx_out, out_sem).wait()
 
 
 def per_device(queries, keys_values, token_ids, lengths, suffix_queries, suffix_kv):
@@ -603,7 +585,7 @@
         pltpu.VMEM((BLK, HD), bf16),
         pltpu.VMEM((2, BLK, HD), bf16),
         pltpu.VMEM((2, BLK, HD), bf16),
-        pltpu.VMEM((3, 8, HSZ), jnp.int32),
+        pltpu.VMEM((24, HSZ), jnp.int32),
         pltpu.VMEM((2, HSZ, GH * HSZ), bf16),
         pltpu.VMEM((NX, NX, GH, QB, HSZ), bf16),
         pltpu.VMEM((2, BLK, HD), bf16),
@@ -628,31 +610,32 @@
         pltpu.VMEM((NZ - 1, 8, HSZ), f32),
         pltpu.VMEM((HSZ, HSZ), f32),
         pltpu.VMEM((HEADS, BLK, HSZ), bf16),
-        dma((9,)),
+        pltpu.VMEM((SHARE, GH * HSZ), bf16),
+        dma((5,)),
         dma, dma, dma, dma,
-        dma((NZ - 1,)), dma((NZ - 1,)),
-        dma((NX - 1,)), dma((NX - 1,)),
-        dma((NX - 1, NX)), dma((NX - 1, NX)),
-        dma((NCH, 2 * NX)), dma((NCH,)), dma((NCH,)),
-        dma((NCH, NX - 1)), dma((NCH,)),
-        dma((NCH, NZ - 1)), dma((NCH,)),
-        dma((NCH, NX - 1)), dma((NCH, NX - 1)),
-        dma((NCH, NX - 1)), dma((NCH, NX - 1)),
-        dma((NCH,)), dma((NCH,)),
-        dma((2, NX - 1, NX)), dma((2, NX - 1, NX)),
-        dma((2, NX - 1)), dma((2, NX - 1)),
-        dma((2, NZ - 1)), dma((2, NZ - 1)),
-        dma((HEADS,)),
+        dma, dma,
+        dma, dma,
+        dma, dma((NX - 1, NX)),
+        dma, dma((NCH,)), dma((NCH,)),
+        dma, dma((NCH,)),
+        dma, dma((NCH,)),
+        dma, dma((NCH,)),
+        dma, dma((NCH,)),
+        dma, dma((NCH,)),
+        dma((2,)), dma((2, NX)),
+        dma((2,)), dma((2,)),
+        dma((2,)), dma((2,)),
+        dma, dma,
     ]
     anywhere = pl.BlockSpec(memory_space=pl.ANY)
     return pl.pallas_call(
         kernel,
         out_shape=(
-            jax.ShapeDtypeStruct((BLK, HD), bf16),
-            jax.ShapeDtypeStruct((SHARE, GH * HSZ), bf16),
+            pltpu.VMEM((BLK, HD), bf16),
+            pltpu.VMEM((SHARE, GH * HSZ), bf16),
         ),
         in_specs=[anywhere, anywhere, anywhere, pl.BlockSpec(memory_space=pltpu.SMEM), anywhere, anywhere],
-        out_specs=(anywhere, pl.BlockSpec(memory_space=pltpu.VMEM)),
+        out_specs=(anywhere, anywhere),
         scratch_shapes=scratch,
         compiler_params=pltpu.CompilerParams(
             collective_id=0, has_side_effects=True, vmem_limit_bytes=56 * 2**20

time: 73.1 us -> 68.5 us (0.937)
  Pallas kernels: 69.1 us -> 65.3 us
  local copies, waits for them, and re-layouts: 3.26 us -> 1.74 us
    pallas_call x1, Pallas kernels: 69.1 us -> 65.3 us  [per_device(): pl.pallas_call(kernel, out_shape=(pltpu.VMEM((BLK, HD), bf16), pltpu.VMEM...]
    unnamed x4 -> x2, local copies, waits for them, and re-layouts: 3.26 us -> 1.74 us
where the time goes in v3:
time: 68.5 us; the launch traced here: 67.7 us
  Pallas kernels  65.3 us (95%)
  local copies, waits for them, and re-layouts  1.74 us (3%)
    pallas_call x1, Pallas kernels, per_device(): pl.pallas_call(kernel, out_shape=(pltpu.VMEM((BLK, HD), bf16), pltpu.VMEM...  65.3 us
    unnamed x2, local copies, waits for them, and re-layouts  1.74 us

profile of v3, /device:TPU:32, one launch (start us, length us, event | category | flops | bytes accessed | tf_op | source)
XLA Modules:
  0.0 67.7 jit_solution(12343019925827121268)
XLA Ops:
  0.6 65.3 %star.1 = (bf16[512,1536]{1,0:T(8,128)(2,1)S(1)}, bf16[16,384]{1,0:T(8,128)(2,1)S(1)}) custom-call(bf16[512,1536]{1,0:T(8,128)(2,1)} %q_hbm.1, bf16[2,512,1536]{2,1,0:T(8,128)(2,1)} %kv_hbm.1, s32[1024,128]{1,0:T(8,128)} %bitcast.1, s32[256]{0:T(256)} %lens.1, bf16[16,384]{1,0:T(8,128)(2,1)} %sq_hbm.1, bf16[2,16,384]{2,1,0:T(8,128)(2,1)} %skv_hbm.1), custom_call_target="tpu_custom_call" | custom-call | flops 6499999744 | bytes 6500000 | tf_op jit(solution)/shard_map/star/pallas_call | solution.py:631
  66.0 1.1 %copy.10 = bf16[512,1536]{1,0:T(8,128)(2,1)} copy(bf16[512,1536]{1,0:T(8,128)(2,1)S(1)} %get-tuple-element.2) | data formatting | bytes 3145728
  67.1 0.6 copy.11

commit v4 on v3

--- a/solution.py
+++ b/solution.py
@@ -472,10 +472,11 @@
     def _(n):
         for at, event in before.items():
             pl.when(n == at)(event)
-        group, step, late = lax.div(n, 2), 2 * rem(n, 2), jnp.where(n < 4, 0, 3)
-        delta = jnp.where(group < 2, group, 5 - group)
-        deltas = (jnp.where(first, delta, late), jnp.where(first, delta, jnp.where(n < 4, 1, 2)))
-        steps = (jnp.where(first, step, rem(n, 4)), jnp.where(first, step + 1, rem(n, 4)))
+        group, shift = lax.div(n, 2), jnp.where(n < 4, 0, 1)
+        delta, late = jnp.where(group < 2, group, 5 - group), 3 * shift
+        deltas = (jnp.where(first, delta, late), jnp.where(first, delta, 1 + shift))
+        step, place_b = 2 * rem(n, 2) + shift, rem(n + shift, 4)
+        steps = (jnp.where(first, step, place_b), jnp.where(first, rem(step + 1, 4), place_b))
         blocks = [(rem(ca + delta, NX), rem(cb + step, NX)) for delta, step in zip(deltas, steps)]
         for delta, (ia, ib) in zip(deltas, blocks):
 

time: 68.5 us -> 67.5 us (0.985)
  Pallas kernels: 65.3 us -> 63.9 us
    pallas_call x1, Pallas kernels: 65.3 us -> 63.9 us  [per_device(): pl.pallas_call(kernel, out_shape=(pltpu.VMEM((BLK, HD), bf16), pltpu.VMEM...]
where the time goes in v4:
time: 67.5 us; the launch traced here: 66.2 us
  Pallas kernels  63.9 us (95%)
  local copies, waits for them, and re-layouts  1.74 us (3%)
    pallas_call x1, Pallas kernels, per_device(): pl.pallas_call(kernel, out_shape=(pltpu.VMEM((BLK, HD), bf16), pltpu.VMEM...  63.9 us
    unnamed x2, local copies, waits for them, and re-layouts  1.74 us

profile of v4, /device:TPU:32, one launch (start us, length us, event | category | flops | bytes accessed | tf_op | source)
XLA Modules:
  0.0 66.2 jit_solution(16266834641770688202)
XLA Ops:
  0.6 63.9 %star.1 = (bf16[512,1536]{1,0:T(8,128)(2,1)S(1)}, bf16[16,384]{1,0:T(8,128)(2,1)S(1)}) custom-call(bf16[512,1536]{1,0:T(8,128)(2,1)} %q_hbm.1, bf16[2,512,1536]{2,1,0:T(8,128)(2,1)} %kv_hbm.1, s32[1024,128]{1,0:T(8,128)} %bitcast.1, s32[256]{0:T(256)} %lens.1, bf16[16,384]{1,0:T(8,128)(2,1)} %sq_hbm.1, bf16[2,16,384]{2,1,0:T(8,128)(2,1)} %skv_hbm.1), custom_call_target="tpu_custom_call" | custom-call | flops 6499999744 | bytes 6500000 | tf_op jit(solution)/shard_map/star/pallas_call | solution.py:632
  64.5 1.1 %copy.10 = bf16[512,1536]{1,0:T(8,128)(2,1)} copy(bf16[512,1536]{1,0:T(8,128)(2,1)S(1)} %get-tuple-element.2) | data formatting | bytes 3145728
  65.6 0.6 copy.11

commit v5 on v4

--- a/solution.py
+++ b/solution.py
@@ -22,6 +22,7 @@
 SHARE = 16
 QB = NZ * SHARE
 TQ = 256
+EARLY = 2
 NCH = 3
 CW = HD // 2 // NCH
 PROWS = BLK // (NX * NY)
@@ -100,13 +101,10 @@
     for i, b in enumerate((block, sblock, 0)):
         row = pl.multiple_of(lax.div(b, 2) * 8, 8)
         loads.append(pltpu.make_async_copy(tok_hbm.at[pl.ds(row, 8), :], tok_v.at[pl.ds(8 * i, 8), :], in_sem.at[3]))
-    for copy in qloads + loads:
-        copy.start()
-
     barrier = pltpu.get_barrier_semaphore()
-    partners = [sibling]
-    partners += [adev(d) for d in range(1, NX)] + [bdev(d) for d in range(1, NY)]
-    partners += [zdev(d) for d in range(1, NZ)]
+    far_first = (4, 3, 5, 2, 6, 1, 7)
+    partners = [zdev(d) for d in far_first]
+    partners += [dev_of(d) for d in (2, 1, 3) for dev_of in (adev, bdev)] + [sibling]
     for partner in partners:
         pl.semaphore_signal(barrier, inc=1, device_id=partner, device_id_type=MESH)
     is_root = block == 0
@@ -116,105 +114,8 @@
     def _():
         pl.semaphore_signal(barrier, inc=1, device_id=(0, 0), device_id_type=MESH)
 
-    pl.semaphore_wait(barrier, len(partners) + jnp.where(is_root, NY - 1, 0))
-
-    ref = qbuf.at[ca, cb, :, pl.ds(zrow, SHARE), :]
-    pltpu.make_async_copy(ref, ref, in_sem.at[4]).wait()
-    zq = []
-    for d in range(1, NZ):
-        ref = qbuf.at[ca, cb, :, pl.ds(zrow, SHARE), :]
-        zq.append(remote(ref, ref, zq_send, zq_recv, zdev(d)))
-        zq[-1].start()
-
-    kvs_copy = remote(kv_hbm, kvs, kvs_send, kvs_recv, sibling)
-    kvs_copy.start()
-    sk_copy = remote(skv_hbm, ksuf.at[:, pl.ds(SHARE, SHARE), :], sk_send, sk_recv, sibling)
-    sk_copy.start()
-
-    def piece(ref, k, pa, pb, core, rows):
-        row = pl.multiple_of(pa * AROWS + pb * PROWS, PROWS)
-        col = pl.multiple_of(core * (HD // 2) + k * CW, HSZ)
-        return ref.at[:, pl.ds(row, rows), pl.ds(col, CW)]
-
-    def scatter_copy(k, i):
-        core, pa = rem(i, 2), lax.div(i, 2)
-        src = piece(kv_hbm, k, pa, 0, core, AROWS)
-        return remote(src, stage.at[k], sc_send, sc_recv.at[k], place(pa, 0, 0, core))
-
-    def root_own(k):
-        return pltpu.make_async_copy(piece(kv_hbm, k, 0, 0, 0, AROWS), stage.at[k], own_sem.at[k])
-
-    @pl.when(is_root)
-    def _():
-        for k in range(NCH):
-            root_own(k).start()
-            for i in (4, 5, 2, 3, 6, 7, 1):
-                scatter_copy(k, jnp.int32(i)).start()
-
-    def sb_copy(k, d):
-        src = stage.at[k, :, pl.ds(d * PROWS, PROWS), :]
-        return remote(src, piece(anc, k, ca, rem(cb + d, NX), c, PROWS), sb_send, sb_recv.at[k], bdev(d))
-
-    def zb_copy(k, d):
-        ref = piece(anc, k, ca, cb, c, PROWS)
-        return remote(ref, ref, zb_send, zb_recv.at[k], zdev(d))
-
-    def bb_copy(k, pb, d):
-        ref = piece(anc, k, ca, pb, c, PROWS)
-        return remote(ref, ref, bb_send, bb_recv.at[k], bdev(d))
-
-    def ab_copy(k, pa, d):
-        ref = piece(anc, k, pa, 0, c, AROWS)
-        return remote(ref, ref, ab_send, ab_recv.at[k], adev(d))
-
-    def sib_copy(k, core):
-        ref = piece(anc, k, 0, 0, core, BLK)
-        return remote(ref, ref, sib_send, sib_recv.at[k], sibling)
-
-    def anchor_first(k):
-        @pl.when((z == 0) & (cb == 0))
-        def _():
-            @pl.when(is_root)
-            def _():
-                root_own(k).wait()
-
-            @pl.when(jnp.logical_not(is_root))
-            def _():
-                remote(stage.at[k], stage.at[k], sib_send, sc_recv.at[k], sibling).wait_recv()
-
-            for d in (2, 1, 3):
-                sb_copy(k, d).start()
-            row = pl.multiple_of(ca * AROWS, AROWS)
-            col = pl.multiple_of(c * (HD // 2) + k * CW, HSZ)
-            anc[:, pl.ds(row, PROWS), pl.ds(col, CW)] = stage[k, :, 0:PROWS, :]
-
-    def anchor_second(k):
-        @pl.when(z == 0)
-        def _():
-            @pl.when(cb > 0)
-            def _():
-                ref = piece(anc, k, ca, cb, c, PROWS)
-                remote(ref, ref, sib_send, sb_recv.at[k], sibling).wait_recv()
-
-            for d in (4, 3, 5, 2, 6, 1, 7):
-                zb_copy(k, d).start()
-
-    def anchor_z(k):
-        @pl.when(z > 0)
-        def _():
-            zb_copy(k, 1).wait_recv()
-
-        for d in (2, 1, 3):
-            bb_copy(k, cb, d).start()
-
-    def anchor_b(k):
-        received(anc.at[:, pl.ds(0, (NX - 1) * PROWS), pl.ds(0, CW)], bb_recv.at[k])
-        for d in (2, 1, 3):
-            ab_copy(k, ca, d).start()
-
-    def anchor_a(k):
-        received(anc.at[:, pl.ds(0, (NX - 1) * AROWS), pl.ds(0, CW)], ab_recv.at[k])
-        sib_copy(k, c).start()
+    for copy in qloads + loads:
+        copy.start()
 
     pltpu.make_async_copy(tok_hbm.at[pl.ds(0, 24), :], tok_v, in_sem.at[3]).wait()
     flat = lax.broadcasted_iota(jnp.int32, (4, HSZ), 0) * HSZ + lax.broadcasted_iota(jnp.int32, (4, HSZ), 1)
@@ -266,7 +167,111 @@
         m1[h, rows, :] = jnp.broadcast_to(m, (TQ, HSZ))
         acc1[h, rows, :] = jnp.dot(p.astype(jnp.bfloat16), v, preferred_element_type=jnp.float32)
 
-    @pl.loop(0, HEADS // 2)
+    @pl.loop(0, EARLY)
+    def _(t):
+        pipelined([(2 * t + i, tile) for i in range(2) for tile in range(BLK // TQ)], own_scores, own_finish)
+
+    pl.semaphore_wait(barrier, len(partners) + jnp.where(is_root, NY - 1, 0))
+
+    ref = qbuf.at[ca, cb, :, pl.ds(zrow, SHARE), :]
+    pltpu.make_async_copy(ref, ref, in_sem.at[4]).wait()
+    zq = []
+    for d in far_first:
+        ref = qbuf.at[ca, cb, :, pl.ds(zrow, SHARE), :]
+        zq.append(remote(ref, ref, zq_send, zq_recv, zdev(d)))
+        zq[-1].start()
+
+    kvs_copy = remote(kv_hbm, kvs, kvs_send, kvs_recv, sibling)
+    kvs_copy.start()
+    sk_copy = remote(skv_hbm, ksuf.at[:, pl.ds(SHARE, SHARE), :], sk_send, sk_recv, sibling)
+    sk_copy.start()
+
+    def piece(ref, k, pa, pb, core, rows):
+        row = pl.multiple_of(pa * AROWS + pb * PROWS, PROWS)
+        col = pl.multiple_of(core * (HD // 2) + k * CW, HSZ)
+        return ref.at[:, pl.ds(row, rows), pl.ds(col, CW)]
+
+    def scatter_copy(k, i):
+        core, pa = rem(i, 2), lax.div(i, 2)
+        src = piece(kv_hbm, k, pa, 0, core, AROWS)
+        return remote(src, stage.at[k], sc_send, sc_recv.at[k], place(pa, 0, 0, core))
+
+    def root_own(k):
+        return pltpu.make_async_copy(piece(kv_hbm, k, 0, 0, 0, AROWS), stage.at[k], own_sem.at[k])
+
+    @pl.when(is_root)
+    def _():
+        for k in range(NCH):
+            root_own(k).start()
+            for i in (4, 5, 2, 3, 6, 7, 1):
+                scatter_copy(k, jnp.int32(i)).start()
+
+    def sb_copy(k, d):
+        src = stage.at[k, :, pl.ds(d * PROWS, PROWS), :]
+        return remote(src, piece(anc, k, ca, rem(cb + d, NX), c, PROWS), sb_send, sb_recv.at[k], bdev(d))
+
+    def zb_copy(k, d):
+        ref = piece(anc, k, ca, cb, c, PROWS)
+        return remote(ref, ref, zb_send, zb_recv.at[k], zdev(d))
+
+    def bb_copy(k, pb, d):
+        ref = piece(anc, k, ca, pb, c, PROWS)
+        return remote(ref, ref, bb_send, bb_recv.at[k], bdev(d))
+
+    def ab_copy(k, pa, d):
+        ref = piece(anc, k, pa, 0, c, AROWS)
+        return remote(ref, ref, ab_send, ab_recv.at[k], adev(d))
+
+    def sib_copy(k, core):
+        ref = piece(anc, k, 0, 0, core, BLK)
+        return remote(ref, ref, sib_send, sib_recv.at[k], sibling)
+
+    def anchor_first(k):
+        @pl.when((z == 0) & (cb == 0))
+        def _():
+            @pl.when(is_root)
+            def _():
+                root_own(k).wait()
+
+            @pl.when(jnp.logical_not(is_root))
+            def _():
+                remote(stage.at[k], stage.at[k], sib_send, sc_recv.at[k], sibling).wait_recv()
+
+            for d in (2, 1, 3):
+                sb_copy(k, d).start()
+            row = pl.multiple_of(ca * AROWS, AROWS)
+            col = pl.multiple_of(c * (HD // 2) + k * CW, HSZ)
+            anc[:, pl.ds(row, PROWS), pl.ds(col, CW)] = stage[k, :, 0:PROWS, :]
+
+    def anchor_second(k):
+        @pl.when(z == 0)
+        def _():
+            @pl.when(cb > 0)
+            def _():
+                ref = piece(anc, k, ca, cb, c, PROWS)
+                remote(ref, ref, sib_send, sb_recv.at[k], sibling).wait_recv()
+
+            for d in (4, 3, 5, 2, 6, 1, 7):
+                zb_copy(k, d).start()
+
+    def anchor_z(k):
+        @pl.when(z > 0)
+        def _():
+            zb_copy(k, 1).wait_recv()
+
+        for d in (2, 1, 3):
+            bb_copy(k, cb, d).start()
+
+    def anchor_b(k):
+        received(anc.at[:, pl.ds(0, (NX - 1) * PROWS), pl.ds(0, CW)], bb_recv.at[k])
+        for d in (2, 1, 3):
+            ab_copy(k, ca, d).start()
+
+    def anchor_a(k):
+        received(anc.at[:, pl.ds(0, (NX - 1) * AROWS), pl.ds(0, CW)], ab_recv.at[k])
+        sib_copy(k, c).start()
+
+    @pl.loop(EARLY, HEADS // 2)
     def _(t):
         pipelined([(2 * t + i, tile) for i in range(2) for tile in range(BLK // TQ)], own_scores, own_finish)
 

time: 67.5 us -> 67.6 us (level)
  no operation moved by 1% of the time
where the time goes in v5:
time: 67.6 us; the launch traced here: 66.8 us
  Pallas kernels  64.4 us (95%)
  local copies, waits for them, and re-layouts  1.74 us (3%)
    pallas_call x1, Pallas kernels, per_device(): pl.pallas_call(kernel, out_shape=(pltpu.VMEM((BLK, HD), bf16), pltpu.VMEM...  64.4 us
    unnamed x2, local copies, waits for them, and re-layouts  1.74 us

profile of v5, /device:TPU:32, one launch (start us, length us, event | category | flops | bytes accessed | tf_op | source)
XLA Modules:
  0.0 66.8 jit_solution(15909146705921424686)
XLA Ops:
  0.6 64.4 %star.1 = (bf16[512,1536]{1,0:T(8,128)(2,1)S(1)}, bf16[16,384]{1,0:T(8,128)(2,1)S(1)}) custom-call(bf16[512,1536]{1,0:T(8,128)(2,1)} %q_hbm.1, bf16[2,512,1536]{2,1,0:T(8,128)(2,1)} %kv_hbm.1, s32[1024,128]{1,0:T(8,128)} %bitcast.1, s32[256]{0:T(256)} %lens.1, bf16[16,384]{1,0:T(8,128)(2,1)} %sq_hbm.1, bf16[2,16,384]{2,1,0:T(8,128)(2,1)} %skv_hbm.1), custom_call_target="tpu_custom_call" | custom-call | flops 6499999744 | bytes 6500000 | tf_op jit(solution)/shard_map/star/pallas_call | solution.py:637
  65.0 1.1 %copy.10 = bf16[512,1536]{1,0:T(8,128)(2,1)} copy(bf16[512,1536]{1,0:T(8,128)(2,1)S(1)} %get-tuple-element.2) | data formatting | bytes 3145728
  66.2 0.6 copy.11
